TPU v7x, 128 devices: a whole 4x4x4 slice. The times are simulated.
128 devices in a mesh: dp: 16 (over x_hi, z, core), tp: 8 (over y, x_lo).
Axes of the slice: x: 4 (x_hi: 2, x_lo: 2; x = x_hi * 2 + x_lo), y: 4, z: 4, core: 2. Of those that a mesh axis runs over, the one named last changes fastest.
Arguments:
- queries: bfloat16 [12288, 12288], P('dp', 'tp'), may hold values from -60 to 60
- latent: bfloat16 [12288, 576], P(('dp', 'tp')), may hold values from -6 to 6
- segments: int32 [16, 6], replicated, may hold values from 0 to 2, never falling along the last dimension, each value on 1 to 4 neighbouring positions
- offsets: int32 [6], replicated, may hold values from 0 to 15
- w_uk: bfloat16 [64, 128, 512], P('tp'), may hold values from -0.5 to 0.5
- w_uv: bfloat16 [64, 512, 128], P('tp'), may hold values from -0.25 to 0.25
- w_out: bfloat16 [8192, 7168], P('tp'), may hold values from -0.0625 to 0.0625
Outputs:
- layer_out: bfloat16 [12288, 7168], P(('dp', 'tp'))
Inputs may be any that keep to these rules, and one draw needn't show every extreme that they name: `segments`: the request ids of one rank never fall along its blocks, so a request's blocks are consecutive.
All inputs are finite; a program needn't handle non-finite values.
Results may differ from a plain program's by a relative error of at most 0.024.
Values may be sent and summed in bfloat16 or wider, within the bound.
A program may use at most 192 MiB of HBM per device.

v0:
```python
import jax
import jax.numpy as jnp
from jax import lax
from jax.sharding import PartitionSpec as P

NOPE = 128
ROPE = 64
LAT = 512
VH = 128


def passed_along(block, axis, distance):
    devices = range(lax.axis_size(axis))
    route = [((i - distance) % len(devices), i) for i in devices]
    return lax.ppermute(block, axis, route)


def attend(query_rows, keys, allowed, w_uk, w_uv):
    count = query_rows.shape[0]
    heads = w_uk.shape[0]
    scale = (NOPE + ROPE) ** (-0.5)
    split_q = query_rows.reshape(count, heads, NOPE + ROPE)
    q_latent = jnp.einsum(
        "mhn,hnl->hml", split_q[:, :, :NOPE], w_uk, preferred_element_type=jnp.float32
    ).astype(jnp.bfloat16)
    content = keys[:, :LAT]
    rope_keys = keys[:, LAT:]
    scores = jnp.einsum("hml,jl->hmj", q_latent, content, preferred_element_type=jnp.float32)
    scores = (
        scores
        + jnp.einsum(
            "mhr,jr->hmj", split_q[:, :, NOPE:], rope_keys, preferred_element_type=jnp.float32
        )
    ) * scale
    scores = jnp.where(allowed[None], scores, -jnp.inf)
    highest = jnp.max(scores, axis=-1, keepdims=True)
    weights = jnp.exp(scores - highest)
    shares = (weights / jnp.sum(weights, axis=-1, keepdims=True)).astype(jnp.bfloat16)
    o_latent = jnp.einsum(
        "hmj,jl->hml", shares, content, preferred_element_type=jnp.float32
    ).astype(jnp.bfloat16)
    values = jnp.einsum("hml,hlv->mhv", o_latent, w_uv, preferred_element_type=jnp.float32).astype(
        jnp.bfloat16
    )
    return values.reshape(count, heads * VH)


def on_device(queries, latent, segments, offsets, w_uk, w_uv, w_out):
    row_count = queries.shape[0]
    block_count = segments.shape[1]
    block_rows = row_count // block_count
    dp_count = lax.axis_size("dp")
    dp_rank = lax.axis_index("dp")
    level_count = dp_count.bit_length() - 1
    slab = lax.all_gather(latent, "tp", axis=0, tiled=True)
    positions = jnp.arange(row_count, dtype=jnp.int32)
    own_requests = jnp.repeat(segments[dp_rank], block_rows)
    allowed = (own_requests[:, None] == own_requests[None, :]) & (
        positions[None, :] <= positions[:, None]
    )
    moved = attend(queries, slab, allowed, w_uk, w_uv).reshape(
        block_count, block_rows, w_uv.shape[0] * VH
    )
    for level in range(level_count):
        arrived = passed_along(moved, "dp", 1 << level)
        taken = offsets // (1 << level) % 2 == 1
        moved = jnp.where(taken[:, None, None], arrived, moved)
    moved_rows = moved.reshape(row_count, moved.shape[2])
    return lax.psum_scatter(
        jnp.dot(moved_rows, w_out, preferred_element_type=jnp.float32).astype(jnp.bfloat16),
        "tp",
        scatter_dimension=0,
        tiled=True,
    )


def solution(mesh):
    return jax.shard_map(
        on_device,
        mesh=mesh,
        in_specs=(
            P("dp", "tp"),
            P(("dp", "tp"), None),
            P(),
            P(),
            P("tp", None, None),
            P("tp", None, None),
            P("tp", None),
        ),
        out_specs=P(("dp", "tp"), None),
        check_vma=False,
    )
```

profile of v0, /device:TPU:0, one launch (start us, length us, event | category | flops | bytes accessed | tf_op | source)
XLA Modules:
  0.0 482.6 jit_solution(18091587581830831811)
XLA Ops:
  6.5 0.0 copy-start
  6.5 0.0 reduce-scatter.2.cloned.1.call-start
  6.5 1.0 dynamic-slice_reduce_fusion
  7.5 0.1 broadcast_bitcast_fusion
  7.6 1.2 fusion.10
  8.8 34.7 %all_gather.3 = bf16[768,576]{1,0:T(8,128)(2,1)} all-gather(bf16[96,576]{1,0:T(8,128)(2,1)} %param.8), channel_id=1, replica_groups=mesh['dp'=16,'tp'=8] {'tp'}, dimensions={0}, use_global_device_ids=true | all-gather | bytes 995328 | tf_op jit(solution)/shard_map/all_gather | solution.py:55
  43.4 2.8 copy.10
  46.3 0.0 copy-done
  46.3 11.8 %fusion.6 = f32[8,768,768]{1,2,0:T(8,128)} fusion(bf16[8,128,512]{2,1,0:T(8,128)(2,1)S(1)} %copy-done, bf16[768,8,192]{0,2,1:T(8,128)(2,1)S(1)} %bitcast.26, bf16[768,576]{1,0:T(8,128)(2,1)} %all_gather.3), kind=kOutput, calls=%fused_computation.10 | convolution fusion | flops 5640290304 | bytes 22282240 | tf_op jit(solution)/shard_map/hml,jl->hmj/dot_general | solution.py:28
  58.0 12.4 %fusion.2 = f32[8,768,768]{1,2,0:T(8,128)} fusion(f32[8,768,768]{1,2,0:T(8,128)} %fusion.6, pred[768,768]{0,1:T(8,128)(4,1)} %fusion.10, bf16[768,8,192]{0,2,1:T(8,128)(2,1)S(1)} %bitcast.27, bf16[768,576]{1,0:T(8,128)(2,1)} %all_gather.3), kind=kOutput, calls=%fused_computation.3 | convolution fusion | flops 618135552 | bytes 39321600 | tf_op jit(solution)/shard_map/mhr,jr->hmj/dot_general | solution.py:31
  70.5 0.0 copy-start.2
  70.5 13.6 %fusion.29 = f32[8,768]{1,0:T(8,128)S(1)} fusion(f32[8,768,768]{1,2,0:T(8,128)} %fusion.2), kind=kOutput, calls=%fused_computation.57 | output fusion | flops 9437951 | bytes 18898944 | tf_op jit(solution)/shard_map/sub | solution.py:37
  84.1 0.0 copy-done.2
  84.1 19.6 %fusion.16 = bf16[768,8,128]{2,0,1:T(8,128)(2,1)S(1)} fusion(bf16[8,512,128]{2,1,0:T(8,128)(2,1)} %param.12, f32[8,768]{1,0:T(8,128)S(1)} %fusion.29, f32[8,768,768]{1,2,0:T(8,128)} %fusion.2, bf16[768,576]{1,0:T(8,128)(2,1)S(1)} %copy-done.2), kind=kOutput, calls=%fused_computation.21 | convolution fusion | flops 5655239168 | bytes 41181184 | tf_op jit(solution)/shard_map/hml,hlv->mhv/dot_general | solution.py:42
  103.7 0.0 copy-start.3
  103.7 2.2 copy.12
  105.9 2.5 reshape_reshape.3
  108.4 0.3 collective-permute-start
  108.7 0.0 copy-done.3
  108.7 23.4 %collective-permute-done = bf16[6,128,1024]{2,1,0:T(8,128)(2,1)S(1)} collective-permute-done((bf16[6,128,1024]{2,1,0:T(8,128)(2,1)S(1)}, bf16[6,128,1024]{2,1,0:T(8,128)(2,1)S(1)}, u32[]{:S(2)}, u32[]{:S(2)}) %collective-permute-start) | collective-permute-done | bytes 1572896 | tf_op jit(solution)/shard_map/ppermute | solution.py:15
  132.1 0.3 broadcast_select_fusion
  132.4 0.1 collective-permute-start.1
  132.5 35.8 %collective-permute-done.1 = bf16[6,128,1024]{2,1,0:T(8,128)(2,1)S(1)} collective-permute-done((bf16[6,128,1024]{2,1,0:T(8,128)(2,1)S(1)}, bf16[6,128,1024]{2,1,0:T(8,128)(2,1)S(1)}, u32[]{:S(2)}, u32[]{:S(2)}) %collective-permute-start.1) | collective-permute-done | bytes 1572896 | tf_op jit(solution)/shard_map/ppermute | solution.py:15
  168.3 0.2 broadcast_select_fusion.1
  168.6 0.1 collective-permute-start.2
  168.6 35.2 %collective-permute-done.2 = bf16[6,128,1024]{2,1,0:T(8,128)(2,1)S(1)} collective-permute-done((bf16[6,128,1024]{2,1,0:T(8,128)(2,1)S(1)}, bf16[6,128,1024]{2,1,0:T(8,128)(2,1)S(1)}, u32[]{:S(2)}, u32[]{:S(2)}) %collective-permute-start.2) | collective-permute-done | bytes 1572896 | tf_op jit(solution)/shard_map/ppermute | solution.py:15
  203.9 0.2 broadcast_select_fusion.2
  204.1 2.9 collective-permute-start.3
  207.0 29.1 %collective-permute-done.3 = bf16[6,128,1024]{2,1,0:T(8,128)(2,1)S(1)} collective-permute-done((bf16[6,128,1024]{2,1,0:T(8,128)(2,1)S(1)}, bf16[6,128,1024]{2,1,0:T(8,128)(2,1)S(1)}, u32[]{:S(2)}, u32[]{:S(2)}) %collective-permute-start.3) | collective-permute-done | bytes 1572896 | tf_op jit(solution)/shard_map/ppermute | solution.py:15
  236.1 0.2 broadcast_select_fusion.3
  236.4 19.1 %convolution_convert_fusion = bf16[768,7168]{1,0:T(8,128)(2,1)} fusion(bf16[768,1024]{1,0:T(8,128)(2,1)S(1)} %bitcast.28, bf16[1024,7168]{1,0:T(8,128)(2,1)} %param.13), kind=kOutput, calls=%fused_computation.6 | convolution fusion | flops 11279794176 | bytes 27262976 | tf_op jit(solution)/shard_map/dot_general | solution.py:70
  255.4 0.0 copy-start.1
  255.4 0.0 reduce-scatter.2.cloned.1.call-update
  255.4 220.3 %reduce-scatter.2.cloned.1.call-done = bf16[96,7168]{1,0:T(8,128)(2,1)} async-done(((bf16[768,7168]{1,0:T(8,128)(2,1)}), bf16[96,7168]{1,0:T(8,128)(2,1)}) %reduce-scatter.2.cloned.1.call-update) | async-done | bytes 1376272 | tf_op jit(solution)/shard_map/reduce_scatter | solution.py:69
  475.8 0.0 copy-done.1
  (1 shorter events, 0.0 us)
Async XLA Ops:
  6.5 39.7 %copy-start = (bf16[8,128,512]{2,1,0:T(8,128)(2,1)S(1)}, bf16[8,128,512]{2,1,0:T(8,128)(2,1)}, u32[]{:S(2)}) copy-start(bf16[8,128,512]{2,1,0:T(8,128)(2,1)} %param.11) | copy-start | bytes 3145732
  6.5 469.2 %reduce-scatter.2.cloned.1.call-start = ((), (), s32[]{:S(2)}) async-start(), calls=%async_computation.1 | async-start | bytes 12386304 | tf_op jit(solution)/shard_map/reduce_scatter | solution.py:69
  70.5 13.6 %copy-start.2 = (bf16[768,576]{1,0:T(8,128)(2,1)S(1)}, bf16[768,576]{1,0:T(8,128)(2,1)}, u32[]{:S(2)}) copy-start(bf16[768,576]{1,0:T(8,128)(2,1)} %all_gather.3) | copy-start | bytes 2654212
  103.7 5.0 %copy-start.3 = (s32[6]{0:T(128)S(1)}, s32[6]{0:T(128)}, u32[]{:S(2)}) copy-start(s32[6]{0:T(128)} %param.10) | copy-start | bytes 76
  108.4 23.7 %collective-permute-start = (bf16[6,128,1024]{2,1,0:T(8,128)(2,1)S(1)}, bf16[6,128,1024]{2,1,0:T(8,128)(2,1)S(1)}, u32[]{:S(2)}, u32[]{:S(2)}) collective-permute-start(bf16[6,128,1024]{2,1,0:T(8,128)(2,1)S(1)} %reshape_reshape.3), channel_id=1, source_target_pairs={{120,0},{0,8},{8,16},{16,24},{24,32},{32,40},{40,48},{48,56},{56,6... | collective-permute-start | bytes 4718600 | tf_op jit(solution)/shard_map/ppermute | solution.py:15
  132.4 35.9 %collective-permute-start.1 = (bf16[6,128,1024]{2,1,0:T(8,128)(2,1)S(1)}, bf16[6,128,1024]{2,1,0:T(8,128)(2,1)S(1)}, u32[]{:S(2)}, u32[]{:S(2)}) collective-permute-start(bf16[6,128,1024]{2,1,0:T(8,128)(2,1)S(1)} %broadcast_select_fusion), channel_id=1, source_target_pairs={{112,0},{120,8},{0,16},{8,24},{16,32},{24,40},{32,48},{40,56},{48,... | collective-permute-start | bytes 4718600 | tf_op jit(solution)/shard_map/ppermute | solution.py:15
  168.6 35.3 %collective-permute-start.2 = (bf16[6,128,1024]{2,1,0:T(8,128)(2,1)S(1)}, bf16[6,128,1024]{2,1,0:T(8,128)(2,1)S(1)}, u32[]{:S(2)}, u32[]{:S(2)}) collective-permute-start(bf16[6,128,1024]{2,1,0:T(8,128)(2,1)S(1)} %broadcast_select_fusion.1), channel_id=1, source_target_pairs={{96,0},{104,8},{112,16},{120,24},{0,32},{8,40},{16,48},{24,56},{32... | collective-permute-start | bytes 4718600 | tf_op jit(solution)/shard_map/ppermute | solution.py:15
  204.1 32.0 %collective-permute-start.3 = (bf16[6,128,1024]{2,1,0:T(8,128)(2,1)S(1)}, bf16[6,128,1024]{2,1,0:T(8,128)(2,1)S(1)}, u32[]{:S(2)}, u32[]{:S(2)}) collective-permute-start(bf16[6,128,1024]{2,1,0:T(8,128)(2,1)S(1)} %broadcast_select_fusion.2), channel_id=1, source_target_pairs={{64,0},{72,8},{80,16},{88,24},{96,32},{104,40},{112,48},{120,56},{... | collective-permute-start | bytes 4718600 | tf_op jit(solution)/shard_map/ppermute | solution.py:15
  255.4 220.3 %copy-start.1 = (bf16[8,128,512]{2,1,0:T(8,128)(2,1)S(1)}, bf16[8,128,512]{2,1,0:T(8,128)(2,1)}, u32[]{:S(2)}) copy-start(bf16[8,128,512]{2,1,0:T(8,128)(2,1)} %param.11) | copy-start | bytes 3145732
Sparse Core Ops, SparseCore 0:
  255.6 220.1 reduce-scatter.1
where the time goes:
time: 484 us; the launch traced here: 483 us
  waiting for transfers between devices  344 us (71%)
  matrix products  62.9 us (13%)
  blocking collectives  34.7 us (7%)
  other arithmetic  15.7 us (3%)
  between operations  13.5 us (3%)
  local copies, waits for them, and re-layouts  8.6 us (2%)
    reduce_scatter x1, waiting for transfers between devices, on_device(): lax.psum_scatter(jnp.dot(moved_rows, w_out, preferred_element_type=jnp.fl...  220 us
    ppermute x4, waiting for transfers between devices, passed_along(): return lax.ppermute(block, axis, route)  124 us
    all_gather x1, blocking collectives, on_device(): slab = lax.all_gather(latent, 'tp', axis=0, tiled=True)  34.7 us
    dot_general x1, matrix products, attend(): jnp.einsum('hml,hlv->mhv', o_latent, w_uv, preferred_element_type=jnp.flo...  19.6 us
    dot_general x1, matrix products, on_device(): jnp.dot(moved_rows, w_out, preferred_element_type=jnp.float32)  19.1 us
    sub x1, other arithmetic, attend(): weights = jnp.exp(scores - highest)  13.6 us
    dot_general x1, matrix products, attend(): jnp.einsum('mhr,jr->hmj', split_q[:, :, NOPE:], rope_keys, preferred_elem...  12.4 us
    dot_general x1, matrix products, attend(): jnp.einsum('hml,jl->hmj', q_latent, content, preferred_element_type=jnp.f...  11.8 us
  transfers between devices with their start and end apart: 5, of which 5 were waited for; matrix products, arithmetic and copies ran while one was open for 0% of the time, Pallas kernels for 0%

commit v1 on v0

v1 whole, which is shorter than its diff:
```python
import functools

import jax
import jax.numpy as jnp
from jax import lax
from jax.experimental import pallas as pl
from jax.experimental.pallas import tpu as pltpu
from jax.sharding import PartitionSpec as P

NOPE = 128
ROPE = 64
LAT = 512
VH = 128
BLK = 128
NB = 6
DP = 16
TP = 8
HEADS = 8
ROWS = NB * BLK
KV = LAT + ROPE
D = 7168
OWN = ROWS // TP
WINDOW = 4
UNIT = 32
PART = 256
SCALE = (NOPE + ROPE) ** (-0.5)
LOG2E = 1.4426950408889634

CHUNK = 512
CHUNKS = D // CHUNK
HALF = CHUNK // 2
W_SLOTS = 3
X_LAG = 2
Y1_LAG = 3
Y2_LAG = 5
ACC_SLOTS = Y2_LAG + 1

MESH = pl.DeviceIdType.MESH
BF16 = jnp.bfloat16
F32 = jnp.float32


def ranks():
    return lax.axis_index("dp"), lax.axis_index("tp")


def remote(src, dst, send, recv, dp, tp):
    return pltpu.make_async_remote_copy(
        src_ref=src,
        dst_ref=dst,
        send_sem=send,
        recv_sem=recv,
        device_id={"dp": dp, "tp": tp},
        device_id_type=MESH,
    )


def greet(peers):
    barrier = pltpu.get_barrier_semaphore()
    for dp, tp in peers:
        pl.semaphore_signal(
            barrier, inc=1, device_id={"dp": dp, "tp": tp}, device_id_type=MESH
        )
    pl.semaphore_wait(barrier, len(peers))


def nt_dot(a, b):
    return lax.dot_general(a, b, (((1,), (1,)), ((), ())), preferred_element_type=F32)


def write_bias(seg_ref, bias, dp):
    row = lax.broadcasted_iota(jnp.int32, (BLK, BLK), 0)
    col = lax.broadcasted_iota(jnp.int32, (BLK, BLK), 1)
    for qb in range(NB):
        first = max(0, qb - WINDOW + 1)
        for kb in range(first, qb + 1):
            if kb == qb:
                block = jnp.where(col <= row, 0.0, -jnp.inf).astype(F32)
            else:
                same = seg_ref[dp, kb] == seg_ref[dp, qb]
                block = jnp.full((BLK, BLK), jnp.where(same, 0.0, -jnp.inf), F32)
            bias[qb, :, (kb - first) * BLK : (kb - first + 1) * BLK] = block


def attend_pair(pair, slab, rope_even, rope_odd, bias, q_ref, wuk_ref, wuv_ref, keys, values, y_ref):
    content = slab[:, :, :LAT].reshape(ROWS, LAT)
    up = wuk_ref[pl.ds(2 * pair, 2)].reshape(2 * NOPE, LAT)
    both = nt_dot(content, up)
    lane = lax.broadcasted_iota(jnp.int32, (ROWS, NOPE), 1)
    keys[0, :, :NOPE] = both[:, :NOPE].astype(BF16)
    keys[0, :, NOPE:] = rope_even[...]
    turned = pltpu.roll(both[:, NOPE:], 64, 1)
    keys[1, :, :NOPE] = jnp.where(lane < 64, 0.0, turned).astype(BF16)
    keys[1, :, NOPE:] = jnp.where(lane < 64, turned, rope_odd[...].astype(F32)).astype(BF16)
    for e in range(2):
        values[:, e * VH : (e + 1) * VH] = jnp.dot(
            content, wuv_ref[2 * pair + e], preferred_element_type=F32
        ).astype(BF16)
    for qb in range(NB):
        first = max(0, qb - WINDOW + 1)
        keep = pl.ds(first * BLK, (qb - first + 1) * BLK)
        for e in range(2):
            start = pl.multiple_of(pair * 384 + 128 * e, 128)
            q = q_ref[pl.ds(qb * BLK, BLK), pl.ds(start, 256)]
            s = nt_dot(q, keys[e, keep, :])
            s = s + bias[qb, :, : (qb - first + 1) * BLK]
            top = jnp.max(s, axis=1, keepdims=True)
            p = jnp.exp2((s - top) * (SCALE * LOG2E))
            total = jnp.sum(p, axis=1, keepdims=True)
            o = jnp.dot(
                p.astype(BF16), values[keep, e * VH : (e + 1) * VH], preferred_element_type=F32
            )
            o = (o / total).astype(BF16)
            for part in range(4):
                y_ref[4 * pair + part, qb, :, e * VH : (e + 1) * VH] = o[
                    part * UNIT : (part + 1) * UNIT
                ]


def attend_kernel(
    seg_ref, lat_ref, q_hbm, wuk_hbm, wuv_hbm, y_ref,
    slab, q_ref, wuk_ref, wuv_ref, rope_even, rope_odd, bias, keys, values,
    send_sem, recv_sem, own_sem,
):
    dp, tp = ranks()
    loads = [
        pltpu.make_async_copy(lat_ref, slab.at[tp], own_sem.at[0]),
        pltpu.make_async_copy(wuk_hbm, wuk_ref, own_sem.at[1]),
        pltpu.make_async_copy(wuv_hbm, wuv_ref, own_sem.at[2]),
        pltpu.make_async_copy(q_hbm, q_ref, own_sem.at[3]),
    ]
    for load in loads:
        load.start()
    greet([(dp, lax.rem(tp + o, TP)) for o in range(1, TP)])
    sends = []
    for o in range(1, TP):
        copy = remote(
            lat_ref, slab.at[tp], send_sem.at[o - 1], recv_sem.at[o - 1], dp, lax.rem(tp + o, TP)
        )
        copy.start()
        sends.append(copy)
    write_bias(seg_ref, bias, dp)
    for load in loads:
        load.wait()
    for o, copy in enumerate(sends):
        copy.wait_recv()
    rope = slab[:, :, LAT:].reshape(ROWS, ROPE)
    blank = jnp.zeros((ROWS, ROPE), BF16)
    rope_even[...] = jnp.concatenate([rope, blank], axis=1)
    rope_odd[...] = jnp.concatenate([blank, rope], axis=1)

    def step(pair, carry):
        attend_pair(
            pair, slab, rope_even, rope_odd, bias, q_ref, wuk_ref, wuv_ref, keys, values, y_ref
        )
        return carry

    lax.fori_loop(0, HEADS // 2, step, 0)
    for copy in sends:
        copy.wait_send()


def attend(segments, latent, queries, w_uk, w_uv):
    any_spec = pl.BlockSpec(memory_space=pl.ANY)
    return pl.pallas_call(
        attend_kernel,
        out_shape=jax.ShapeDtypeStruct((DP, NB, UNIT, PART), BF16),
        in_specs=[pl.BlockSpec(memory_space=pltpu.SMEM)] + [any_spec] * 4,
        out_specs=pl.BlockSpec(memory_space=pltpu.VMEM),
        scratch_shapes=[
            pltpu.VMEM((TP, OWN, KV), BF16),
            pltpu.VMEM((ROWS, HEADS * (NOPE + ROPE)), BF16),
            pltpu.VMEM((HEADS, NOPE, LAT), BF16),
            pltpu.VMEM((HEADS, LAT, VH), BF16),
            pltpu.VMEM((ROWS, 2 * ROPE), BF16),
            pltpu.VMEM((ROWS, 2 * ROPE), BF16),
            pltpu.VMEM((NB, BLK, WINDOW * BLK), F32),
            pltpu.VMEM((2, ROWS, 2 * NOPE), BF16),
            pltpu.VMEM((ROWS, 2 * VH), BF16),
            pltpu.SemaphoreType.DMA((TP - 1,)),
            pltpu.SemaphoreType.DMA((TP - 1,)),
            pltpu.SemaphoreType.DMA((4,)),
        ],
        compiler_params=pltpu.CompilerParams(
            collective_id=0, has_side_effects=True, vmem_limit_bytes=40 * 2**20
        ),
        name="gather_attend",
    )(segments, latent, queries, w_uk, w_uv)


def pick(off_ref, me, lo, d, k):
    unit = 4 * k + lax.rem(me, 4)
    crossed = (lax.rem(unit // 6, 2) == 1) & (lax.rem(unit // 3, 2) != lo)
    rank = d + jnp.where(crossed, DP // 2, 0)
    return lax.rem(rank + DP - off_ref[k], DP)


def migrate_kernel(off_ref, y_ref, z_ref, gathered, staged, send1, recv1, send2, recv2, own_sem):
    dp, tp = ranks()
    lo = lax.rem(tp, 2)
    own = pltpu.make_async_copy(y_ref.at[dp], gathered.at[dp], own_sem)
    own.start()
    greet([(lax.rem(dp + o, DP), tp) for o in range(1, DP)])
    firsts = []
    for o in range(1, DP):
        peer = lax.rem(dp + o, DP)
        copy = remote(
            y_ref.at[peer], gathered.at[dp], send1.at[o - 1], recv1.at[o - 1], peer, tp
        )
        copy.start()
        firsts.append(copy)
    own.wait()
    for copy in firsts:
        copy.wait_recv()
    seconds = []
    for o in range(1, DP):
        peer = lax.rem(dp + o, DP)
        for k in range(NB):
            staged[o, k] = gathered[pick(off_ref, dp, lo, peer, k), k]
        copy = remote(
            staged.at[o], z_ref.at[dp], send2.at[o - 1], recv2.at[o - 1], peer, tp
        )
        copy.start()
        seconds.append(copy)
    for k in range(NB):
        z_ref[dp, k] = gathered[pick(off_ref, dp, lo, dp, k), k]
    for copy in seconds:
        copy.wait_recv()
    for copy in firsts + seconds:
        copy.wait_send()


def migrate(offsets, parts):
    return pl.pallas_call(
        migrate_kernel,
        out_shape=jax.ShapeDtypeStruct((DP, NB, UNIT, PART), BF16),
        in_specs=[
            pl.BlockSpec(memory_space=pltpu.SMEM),
            pl.BlockSpec(memory_space=pltpu.VMEM),
        ],
        out_specs=pl.BlockSpec(memory_space=pltpu.VMEM),
        scratch_shapes=[
            pltpu.VMEM((DP, NB, UNIT, PART), BF16),
            pltpu.VMEM((DP, NB, UNIT, PART), BF16),
            pltpu.SemaphoreType.DMA((DP - 1,)),
            pltpu.SemaphoreType.DMA((DP - 1,)),
            pltpu.SemaphoreType.DMA((DP - 1,)),
            pltpu.SemaphoreType.DMA((DP - 1,)),
            pltpu.SemaphoreType.DMA,
        ],
        compiler_params=pltpu.CompilerParams(
            collective_id=1, has_side_effects=True, vmem_limit_bytes=40 * 2**20
        ),
        name="migrate",
    )(offsets, parts)


def slot_of(y):
    return lax.rem(y, 2) * 2 + y // 2


def project_kernel(
    z_ref, w_ref, out_ref,
    rows, w_buf, acc, x_out, x_in, y1_out, y1_in, y2_out, y2_in,
    w_sem, xs_sem, xr_sem, y1s_sem, y1r_sem, y2s_sem, y2r_sem,
):
    dp, tp = ranks()
    y, lo = tp // 2, lax.rem(tp, 2)
    other_dp = lax.rem(dp + DP // 2, DP)
    across = 2 * y + 1 - lo
    up_y, down_y, far_y = lax.rem(y + 1, 4), lax.rem(y + 3, 4), lax.rem(y + 2, 4)
    up, down = 2 * up_y + lo, 2 * down_y + lo

    def load(c):
        start = pl.multiple_of(c * CHUNK, CHUNK)
        slot = lax.rem(c, W_SLOTS)
        return pltpu.make_async_copy(
            w_ref.at[:, pl.ds(start, CHUNK)], w_buf.at[slot], w_sem.at[slot]
        )

    def x_copies(c):
        return [
            remote(x_out.at[c, 0], x_in.at[c, 0], xs_sem.at[c, 0], xr_sem.at[c, 0], dp, across),
            remote(x_out.at[c, 1], x_in.at[c, 1], xs_sem.at[c, 1], xr_sem.at[c, 1], other_dp, across),
        ]

    def y1_copies(c):
        return [
            remote(y1_out.at[c, 0], y1_in.at[c, 0], y1s_sem.at[c, 0], y1r_sem.at[c, 0], dp, up),
            remote(y1_out.at[c, 1], y1_in.at[c, 1], y1s_sem.at[c, 1], y1r_sem.at[c, 1], dp, down),
        ]

    def y2_copies(c):
        return [
            remote(y2_out.at[c, 0], y2_in.at[c, 0], y2s_sem.at[c, 0], y2r_sem.at[c, 0], dp, up),
            remote(y2_out.at[c, 1], y2_in.at[c, 1], y2s_sem.at[c, 1], y2r_sem.at[c, 1], dp, down),
        ]

    for c in range(W_SLOTS - 1):
        load(c).start()
    for unit in range(ROWS // UNIT):
        t, third = unit // 3, unit % 3
        yp, lop = t // 2, t % 2
        at = (yp % 2) * 2 + yp // 2
        for pair in range(4):
            rows[lop, at, pl.ds(third * UNIT, UNIT), pl.ds(pair * PART, PART)] = z_ref[
                4 * pair + unit % 4, unit // 4
            ]
    greet([(dp, across), (other_dp, across), (dp, up), (dp, down)])

    def step(i, carry):
        @pl.when(i < CHUNKS)
        def _():
            slot = lax.rem(i, W_SLOTS)
            load(i).wait()

            @pl.when(i + W_SLOTS - 1 < CHUNKS)
            def _():
                load(i + W_SLOTS - 1).start()

            w = w_buf[slot]
            x_out[i] = (
                jnp.dot(rows[1 - lo].reshape(4 * OWN, TP * VH), w, preferred_element_type=F32)
                .astype(BF16)
                .reshape(2, 2, OWN, CHUNK)
            )
            for copy in x_copies(i):
                copy.start()
            acc[lax.rem(i, ACC_SLOTS)] = jnp.dot(
                rows[lo].reshape(4 * OWN, TP * VH), w, preferred_element_type=F32
            ).reshape(4, OWN, CHUNK)

        @pl.when((i >= X_LAG) & (i < CHUNKS + X_LAG))
        def _():
            c = i - X_LAG
            slot = lax.rem(c, ACC_SLOTS)
            for copy in x_copies(c):
                copy.wait_recv()
            acc[slot] = acc[slot] + x_in[c].reshape(4, OWN, CHUNK).astype(F32)
            far = acc[slot, slot_of(far_y)].astype(BF16)
            y1_out[c, 0] = far[:, :HALF]
            y1_out[c, 1] = far[:, HALF:]
            for copy in y1_copies(c):
                copy.start()

        @pl.when((i >= Y1_LAG) & (i < CHUNKS + Y1_LAG))
        def _():
            c = i - Y1_LAG
            slot = lax.rem(c, ACC_SLOTS)
            for copy in y1_copies(c):
                copy.wait_recv()
            to_up = acc[slot, slot_of(up_y)]
            y2_out[c, 0, :, :HALF] = (to_up[:, :HALF] + y1_in[c, 0].astype(F32)).astype(BF16)
            y2_out[c, 0, :, HALF:] = to_up[:, HALF:].astype(BF16)
            to_down = acc[slot, slot_of(down_y)]
            y2_out[c, 1, :, :HALF] = to_down[:, :HALF].astype(BF16)
            y2_out[c, 1, :, HALF:] = (to_down[:, HALF:] + y1_in[c, 1].astype(F32)).astype(BF16)
            for copy in y2_copies(c):
                copy.start()

        @pl.when((i >= Y2_LAG) & (i < CHUNKS + Y2_LAG))
        def _():
            c = i - Y2_LAG
            slot = lax.rem(c, ACC_SLOTS)
            for copy in y2_copies(c):
                copy.wait_recv()
            start = pl.multiple_of(c * CHUNK, CHUNK)
            out_ref[:, pl.ds(start, CHUNK)] = (
                acc[slot, slot_of(y)] + y2_in[c, 0].astype(F32) + y2_in[c, 1].astype(F32)
            ).astype(BF16)

        return carry

    lax.fori_loop(0, CHUNKS + Y2_LAG, step, 0)

    def drain(c, carry):
        for copy in x_copies(c) + y1_copies(c) + y2_copies(c):
            copy.wait_send()
        return carry

    lax.fori_loop(0, CHUNKS, drain, 0)


def project(moved, w_out):
    pairs = pltpu.SemaphoreType.DMA((CHUNKS, 2))
    return pl.pallas_call(
        project_kernel,
        out_shape=jax.ShapeDtypeStruct((OWN, D), BF16),
        in_specs=[
            pl.BlockSpec(memory_space=pltpu.VMEM),
            pl.BlockSpec(memory_space=pl.ANY),
        ],
        out_specs=pl.BlockSpec(memory_space=pltpu.VMEM),
        scratch_shapes=[
            pltpu.VMEM((2, 4, OWN, TP * VH), BF16),
            pltpu.VMEM((W_SLOTS, TP * VH, CHUNK), BF16),
            pltpu.VMEM((ACC_SLOTS, 4, OWN, CHUNK), F32),
            pltpu.VMEM((CHUNKS, 2, 2, OWN, CHUNK), BF16),
            pltpu.VMEM((CHUNKS, 2, 2, OWN, CHUNK), BF16),
            pltpu.VMEM((CHUNKS, 2, OWN, HALF), BF16),
            pltpu.VMEM((CHUNKS, 2, OWN, HALF), BF16),
            pltpu.VMEM((CHUNKS, 2, OWN, CHUNK), BF16),
            pltpu.VMEM((CHUNKS, 2, OWN, CHUNK), BF16),
            pltpu.SemaphoreType.DMA((W_SLOTS,)),
        ]
        + [pairs] * 6,
        compiler_params=pltpu.CompilerParams(
            collective_id=2, has_side_effects=True, vmem_limit_bytes=56 * 2**20
        ),
        name="project",
    )(moved, w_out)


def on_device(queries, latent, segments, offsets, w_uk, w_uv, w_out):
    parts = attend(segments, latent, queries, w_uk, w_uv)
    moved = migrate(offsets, parts)
    return project(moved, w_out)


def solution(mesh):
    return jax.shard_map(
        on_device,
        mesh=mesh,
        in_specs=(
            P("dp", "tp"),
            P(("dp", "tp"), None),
            P(),
            P(),
            P("tp", None, None),
            P("tp", None, None),
            P("tp", None),
        ),
        out_specs=P(("dp", "tp"), None),
        check_vma=False,
    )
```

time: 484 us -> 173 us (0.36)
  waiting for transfers between devices: 344 us -> 0 us
  Pallas kernels: 0 us -> 160 us
  matrix products: 62.9 us -> 0 us
  blocking collectives: 34.7 us -> 0 us
  other arithmetic: 15.7 us -> 0 us
  between operations: 13.5 us -> 0.05 us
    reduce_scatter x1 -> x0, waiting for transfers between devices: 220 us -> none  [on_device(): lax.psum_scatter(jnp.dot(moved_rows, w_out, preferred_element_type=jnp.fl...]
    pallas_call x0 -> x3, Pallas kernels: none -> 160 us  [the longest x1 78.1 us: project(): pl.pallas_call(project_kernel, out_shape=jax.ShapeDtypeStruct((OWN, D), B...]
    ppermute x4 -> x0, waiting for transfers between devices: 124 us -> none  [passed_along(): return lax.ppermute(block, axis, route)]
    dot_general x4 -> x0, matrix products: 62.9 us -> none  [the longest x1 19.6 us: attend(): jnp.einsum('hml,hlv->mhv', o_latent, w_uv, preferred_element_type=jnp.flo...]
    all_gather x1 -> x0, blocking collectives: 34.7 us -> none  [on_device(): slab = lax.all_gather(latent, 'tp', axis=0, tiled=True)]
    sub x1 -> x0, other arithmetic: 13.6 us -> none  [attend(): weights = jnp.exp(scores - highest)]
    unnamed x9 -> x14, local copies, waits for them, and re-layouts: 2.85 us -> 9.44 us
  transfers between devices with their start and end apart: 5 -> 0, of which waited for: 5 -> 0; matrix products, arithmetic and copies ran while one was open for 0% -> 0% of each run, Pallas kernels for 0% -> 0%
where the time goes in v1:
time: 173 us; the launch traced here: 170 us
  Pallas kernels  160 us (92%)
  local copies, waits for them, and re-layouts  9.44 us (5%)
    pallas_call x1, Pallas kernels, project(): pl.pallas_call(project_kernel, out_shape=jax.ShapeDtypeStruct((OWN, D), B...  78.1 us
    pallas_call x1, Pallas kernels, migrate(): pl.pallas_call(migrate_kernel, out_shape=jax.ShapeDtypeStruct((DP, NB, UN...  48 us
    pallas_call x1, Pallas kernels, attend(): pl.pallas_call(attend_kernel, out_shape=jax.ShapeDtypeStruct((DP, NB, UNI...  34.1 us
    unnamed x14, local copies, waits for them, and re-layouts  9.44 us

profile of v1, /device:TPU:0, one launch (start us, length us, event | category | flops | bytes accessed | tf_op | source)
XLA Modules:
  0.0 169.7 jit_solution(6594919036875990747)
XLA Ops:
  0.0 0.8 copy.8.seg_ref
  0.8 0.0 copy-start.1
  0.8 1.7 copy-done.1
  2.4 0.0 copy-start.2
  2.4 1.2 copy-done.2
  3.7 0.0 copy-start.3
  3.7 1.2 copy-done.3
  4.9 0.0 copy-start.4
  4.9 0.9 copy-done.4
  5.8 0.0 copy-start.5
  5.8 34.1 %gather_attend.1.y_ref = bf16[16,6,32,256]{3,2,1,0:T(8,128)(2,1)S(1)} custom-call(s32[16,6]{1,0:T(8,128)S(1)} %copy.8.seg_ref, bf16[96,576]{1,0:T(8,128)(2,1)S(1)} %copy-done.4, bf16[768,1536]{1,0:T(8,128)(2,1)S(1)} %copy-done.1, bf16[8,128,512]{2,1,0:T(8,128)(2,1)S(1)} %copy-done.2, bf16[8,512,128]{2,1,0:T(8,128)(2,1)S(1)} %copy-done.3), custom_call_target="tpu_custom_call" | custom-call | tf_op jit(solution)/shard_map/gather_attend/pallas_call | solution.py:165
  39.9 0.0 copy-done.5
  39.9 48.0 %migrate.1.z_ref = bf16[16,6,32,256]{3,2,1,0:T(8,128)(2,1)S(1)} custom-call(s32[6]{0:T(128)S(1)} %copy-done.5, bf16[16,6,32,256]{3,2,1,0:T(8,128)(2,1)S(1)} %gather_attend.1.y_ref), custom_call_target="tpu_custom_call" | custom-call | tf_op jit(solution)/shard_map/migrate/pallas_call | solution.py:234
  88.0 0.0 copy-start
  88.0 1.1 copy-done
  89.1 78.1 %project.1 = bf16[96,7168]{1,0:T(8,128)(2,1)} custom-call(bf16[16,6,32,256]{3,2,1,0:T(8,128)(2,1)} %copy-done, bf16[1024,7168]{1,0:T(8,128)(2,1)} %w_ref.1), custom_call_target="tpu_custom_call" | custom-call | tf_op jit(solution)/shard_map/project/pallas_call | solution.py:386
  167.2 2.5 %copy.10 = bf16[96,7168]{1,0:T(8,128)(2,1)} copy(bf16[96,7168]{1,0:T(8,128)(2,1)} %project.1) | data formatting | bytes 2752512
Async XLA Ops:
  0.8 1.7 copy-start.1
  2.4 1.2 copy-start.2
  3.7 1.2 copy-start.3
  4.9 0.9 copy-start.4
  5.8 34.2 %copy-start.5 = (s32[6]{0:T(128)S(1)}, s32[6]{0:T(128)}, u32[]{:S(2)}) copy-start(s32[6]{0:T(128)} %off_ref.1) | copy-start | bytes 76
  88.0 1.2 copy-start

commit v2 on v1

v2 whole, which is shorter than its diff:
```python
import functools

import jax
import jax.numpy as jnp
from jax import lax
from jax.experimental import pallas as pl
from jax.experimental.pallas import tpu as pltpu
from jax.sharding import PartitionSpec as P

NOPE = 128
ROPE = 64
LAT = 512
VH = 128
BLK = 128
NB = 6
DP = 16
TP = 8
HEADS = 8
ROWS = NB * BLK
KV = LAT + ROPE
D = 7168
OWN = ROWS // TP
PARTS = 4
PAIRS = HEADS // 2
WINDOW = 4
UNIT = 32
PART = 256
SCALE = (NOPE + ROPE) ** (-0.5)
LOG2E = 1.4426950408889634

CHUNK = 512
CHUNKS = D // CHUNK
HALF = CHUNK // 2
W_SLOTS = 3
X_LAG = 2
Y1_LAG = 3
Y2_LAG = 5
ACC_SLOTS = Y2_LAG + 1

MESH = pl.DeviceIdType.MESH
BF16 = jnp.bfloat16
F32 = jnp.float32


def ranks():
    return lax.axis_index("dp"), lax.axis_index("tp")


def remote(src, dst, send, recv, dp, tp):
    return pltpu.make_async_remote_copy(
        src_ref=src,
        dst_ref=dst,
        send_sem=send,
        recv_sem=recv,
        device_id={"dp": dp, "tp": tp},
        device_id_type=MESH,
    )


def greet(peers):
    barrier = pltpu.get_barrier_semaphore()
    for dp, tp in peers:
        pl.semaphore_signal(
            barrier, inc=1, device_id={"dp": dp, "tp": tp}, device_id_type=MESH
        )
    pl.semaphore_wait(barrier, len(peers))


def nt_dot(a, b):
    return lax.dot_general(a, b, (((1,), (1,)), ((), ())), preferred_element_type=F32)


HOME = ((3, 11, 6), (4, 0, 5), (9, 1, 7), (10, 2, 8))


def unit_of(p, e, u):
    y, third = divmod(HOME[p][u], 3)
    unit = 6 * y + third
    return 23 - unit if e else unit


PLACE = {
    unit_of(p, e, u): (p, e, u) for p in range(PARTS) for e in range(2) for u in range(3)
}


def block_of(p, e, u):
    first = (
        jnp.where(p < 2, 1, 4),
        jnp.where(p == 0, 5, 0),
        jnp.where(p == 1, 2, 3),
    )[u]
    return jnp.where(e == 1, NB - 1 - first, first)


def write_bias(seg_ref, bias, dp):
    row = lax.broadcasted_iota(jnp.int32, (BLK, BLK), 0)
    col = lax.broadcasted_iota(jnp.int32, (BLK, BLK), 1)
    for qb in range(NB):
        first = max(0, qb - WINDOW + 1)
        for kb in range(first, qb + 1):
            if kb == qb:
                block = jnp.where(col <= row, 0.0, -jnp.inf).astype(F32)
            else:
                same = seg_ref[dp, kb] == seg_ref[dp, qb]
                block = jnp.full((BLK, BLK), jnp.where(same, 0.0, -jnp.inf), F32)
            bias[qb, :, (kb - first) * BLK : (kb - first + 1) * BLK] = block


def attend_pair(pair, slab, rope_even, rope_odd, bias, q_ref, wuk_ref, wuv_ref, keys, values, parts):
    content = slab[:, :, :LAT].reshape(ROWS, LAT)
    up = wuk_ref[pl.ds(2 * pair, 2)].reshape(2 * NOPE, LAT)
    both = nt_dot(content, up)
    lane = lax.broadcasted_iota(jnp.int32, (ROWS, NOPE), 1)
    keys[0, :, :NOPE] = both[:, :NOPE].astype(BF16)
    keys[0, :, NOPE:] = rope_even[...]
    turned = pltpu.roll(both[:, NOPE:], 64, 1)
    keys[1, :, :NOPE] = jnp.where(lane < 64, 0.0, turned).astype(BF16)
    keys[1, :, NOPE:] = jnp.where(lane < 64, turned, rope_odd[...].astype(F32)).astype(BF16)
    for e in range(2):
        values[:, e * VH : (e + 1) * VH] = jnp.dot(
            content, wuv_ref[2 * pair + e], preferred_element_type=F32
        ).astype(BF16)
    for qb in range(NB):
        first = max(0, qb - WINDOW + 1)
        keep = pl.ds(first * BLK, (qb - first + 1) * BLK)
        for e in range(2):
            start = pl.multiple_of(pair * 384 + 128 * e, 128)
            q = q_ref[pl.ds(qb * BLK, BLK), pl.ds(start, 256)]
            s = nt_dot(q, keys[e, keep, :])
            s = s + bias[qb, :, : (qb - first + 1) * BLK]
            top = jnp.max(s, axis=1, keepdims=True)
            p = jnp.exp2((s - top) * (SCALE * LOG2E))
            total = jnp.sum(p, axis=1, keepdims=True)
            o = jnp.dot(
                p.astype(BF16), values[keep, e * VH : (e + 1) * VH], preferred_element_type=F32
            )
            o = (o / total).astype(BF16)
            for quarter in range(4):
                part, side, u = PLACE[4 * qb + quarter]
                parts[pair, part, side, u, :, e * VH : (e + 1) * VH] = o[
                    quarter * UNIT : (quarter + 1) * UNIT
                ]


def whole_kernel(
    seg_ref, off_ref, lat_hbm, q_hbm, wuk_hbm, wuv_hbm, w_hbm, out_ref,
    slab, q_ref, wuk_ref, wuv_ref, rope_even, rope_odd, bias, keys, values,
    parts, gathered, staged_near, staged_far, near, far, rows_keep, rows_away,
    w_buf, acc, x_out, x_in, y1_out, y1_in, y2_out, y2_in,
    own_sem, ag_s, ag_r, p1_s, p1_r, p2_s, p2_r,
    w_sem, xs_sem, xr_sem, y1s_sem, y1r_sem, y2s_sem, y2r_sem,
):
    dp, tp = ranks()
    y, lo = tp // 2, lax.rem(tp, 2)
    hi, z, core = dp // 8, lax.rem(dp // 2, 4), lax.rem(dp, 2)
    across = 2 * y + 1 - lo
    own_y = jnp.where(lo == 1, 3 - y, y)
    step_y = jnp.where(lo == 1, 3, 1)
    up = 2 * lax.rem(y + step_y, 4) + lo
    down = 2 * lax.rem(y + 4 - step_y, 4) + lo
    up_y, down_y, far_y = lax.rem(own_y + 1, 4), lax.rem(own_y + 3, 4), lax.rem(own_y + 2, 4)

    def flip(bit, by):
        return bit + by - 2 * bit * by

    def rank_at(o, a, b):
        return flip(hi, a) * 8 + lax.rem(z + o, 4) * 2 + flip(core, b)

    def load(c):
        start = pl.multiple_of(c * CHUNK, CHUNK)
        slot = lax.rem(c, W_SLOTS)
        return pltpu.make_async_copy(
            w_hbm.at[:, pl.ds(start, CHUNK)], w_buf.at[slot], w_sem.at[slot]
        )

    loads = [
        pltpu.make_async_copy(lat_hbm, slab.at[tp], own_sem.at[0]),
        pltpu.make_async_copy(wuk_hbm, wuk_ref, own_sem.at[1]),
        pltpu.make_async_copy(wuv_hbm, wuv_ref, own_sem.at[2]),
        pltpu.make_async_copy(q_hbm, q_ref, own_sem.at[3]),
    ]
    for copy in loads:
        copy.start()
    for c in range(W_SLOTS - 1):
        load(c).start()

    greet(
        [(dp, lax.rem(tp + o, TP)) for o in range(1, TP)]
        + [(lax.rem(dp + o, DP), tp) for o in range(1, DP)]
        + [(lax.rem(dp + DP // 2, DP), across)]
    )

    gathers = []
    for o in range(1, TP):
        copy = remote(
            lat_hbm, slab.at[tp], ag_s.at[o - 1], ag_r.at[o - 1], dp, lax.rem(tp + o, TP)
        )
        copy.start()
        gathers.append(copy)
    write_bias(seg_ref, bias, dp)
    for copy in loads:
        copy.wait()
    for copy in gathers:
        copy.wait_recv()
    rope = slab[:, :, LAT:].reshape(ROWS, ROPE)
    blank = jnp.zeros((ROWS, ROPE), BF16)
    rope_even[...] = jnp.concatenate([rope, blank], axis=1)
    rope_odd[...] = jnp.concatenate([blank, rope], axis=1)

    def spread(o, a, b):
        pair = lax.rem(z + o, 4)
        part = 2 * flip(core, b) + flip(hi, a)
        at = o * 4 + a * 2 + b
        return remote(
            parts.at[pair, part], gathered.at[dp], p1_s.at[at], p1_r.at[at], rank_at(o, a, b), tp
        )

    own_part = pltpu.make_async_copy(
        parts.at[z, 2 * core + hi], gathered.at[dp], p1_s.at[0]
    )

    def attend_step(i, carry):
        o = jnp.where(i == 0, 2, jnp.where(i == 1, 1, jnp.where(i == 2, 3, 0)))
        attend_pair(
            lax.rem(z + o, 4), slab, rope_even, rope_odd, bias, q_ref, wuk_ref, wuv_ref,
            keys, values, parts,
        )
        for a, b in ((1, 0), (1, 1), (0, 1)):
            spread(o, a, b).start()

        @pl.when(o != 0)
        def _():
            spread(o, 0, 0).start()

        return carry

    lax.fori_loop(0, PAIRS, attend_step, 0)
    own_part.start()
    ways = [(o, a, b) for o in (2, 1, 3, 0) for a in (1, 0) for b in (1, 0)]
    others = [way for way in ways if way != (0, 0, 0)]
    for way in others:
        spread(*way).wait_recv()
    own_part.wait()

    part = 2 * core + hi
    near_sends, far_sends = [], []

    def taken(rank, e, u):
        source = lax.rem(rank + DP - off_ref[block_of(part, e, u)], DP)
        return gathered[source, e, u]

    def deliver(o, a, b):
        at = o * 4 + a * 2 + b
        src = (staged_far if a else staged_near).at[2 * o + b]
        dst = (far if a else near).at[2 * z + core]
        return remote(src, dst, p2_s.at[at], p2_r.at[at], rank_at(o, a, b), tp)

    for o, a, b in ways:
        rank = rank_at(o, a, b)
        slot = 2 * o + b
        if a:
            target, index = staged_far, slot
        elif (o, b) == (0, 0):
            target, index = near, 2 * z + core
        else:
            target, index = staged_near, slot
        for u in range(3):
            target[index, u] = taken(rank, lo, u)
        if not a:
            for side in range(2):
                for u in range(3):
                    target[index, 3 + 3 * side + u] = taken(
                        rank + (side - hi) * 8, 1 - lo, u
                    )
        if (o, a, b) != (0, 0, 0):
            deliver(o, a, b).start()
    for way in others:
        deliver(*way).wait_recv()

    for pair in range(PAIRS):
        columns = pl.ds(pair * PART, PART)
        for c in range(2):
            for u in range(3):
                for a in range(2):
                    home = jnp.where(hi == 0, HOME[2 * c + a][u], HOME[2 * c + 1 - a][u])
                    rows_keep[home, :, columns] = (far if a else near)[2 * pair + c, u]
                for side in range(2):
                    rows_away[side, 3 * c + u, :, columns] = near[2 * pair + c, 3 + 3 * side + u]

    def x_copies(c):
        return [
            remote(
                x_out.at[c, flip(hi, a)], x_in.at[c, hi], xs_sem.at[c, a], xr_sem.at[c, a],
                rank_at(0, a, 0), across,
            )
            for a in range(2)
        ]

    def y1_copies(c):
        return [
            remote(y1_out.at[c, 0], y1_in.at[c, 0], y1s_sem.at[c, 0], y1r_sem.at[c, 0], dp, up),
            remote(y1_out.at[c, 1], y1_in.at[c, 1], y1s_sem.at[c, 1], y1r_sem.at[c, 1], dp, down),
        ]

    def y2_copies(c):
        return [
            remote(y2_out.at[c, 0], y2_in.at[c, 0], y2s_sem.at[c, 0], y2r_sem.at[c, 0], dp, up),
            remote(y2_out.at[c, 1], y2_in.at[c, 1], y2s_sem.at[c, 1], y2r_sem.at[c, 1], dp, down),
        ]

    def group(slot, at):
        return acc[slot, pl.ds(3 * at, 3)].reshape(OWN, CHUNK)

    def project_step(i, carry):
        @pl.when(i < CHUNKS)
        def _():
            slot = lax.rem(i, W_SLOTS)
            load(i).wait()

            @pl.when(i + W_SLOTS - 1 < CHUNKS)
            def _():
                load(i + W_SLOTS - 1).start()

            w = w_buf[slot]
            x_out[i] = (
                jnp.dot(rows_away[...].reshape(4 * OWN, TP * VH), w, preferred_element_type=F32)
                .astype(BF16)
                .reshape(2, 2 * OWN, CHUNK)
            )
            for copy in x_copies(i):
                copy.start()
            acc[lax.rem(i, ACC_SLOTS)] = jnp.dot(
                rows_keep[...].reshape(4 * OWN, TP * VH), w, preferred_element_type=F32
            ).reshape(12, UNIT, CHUNK)

        @pl.when((i >= X_LAG) & (i < CHUNKS + X_LAG))
        def _():
            c = i - X_LAG
            slot = lax.rem(c, ACC_SLOTS)
            for copy in x_copies(c):
                copy.wait_recv()
            for side in range(2):
                for half in range(2):
                    for u in range(3):
                        home = HOME[2 * half + side][u]
                        acc[slot, home] = acc[slot, home] + x_in[
                            c, side, pl.ds((3 * half + u) * UNIT, UNIT)
                        ].astype(F32)
            other = group(slot, far_y).astype(BF16)
            y1_out[c, 0] = other[:, :HALF]
            y1_out[c, 1] = other[:, HALF:]
            for copy in y1_copies(c):
                copy.start()

        @pl.when((i >= Y1_LAG) & (i < CHUNKS + Y1_LAG))
        def _():
            c = i - Y1_LAG
            slot = lax.rem(c, ACC_SLOTS)
            for copy in y1_copies(c):
                copy.wait_recv()
            to_up = group(slot, up_y)
            y2_out[c, 0, :, :HALF] = (to_up[:, :HALF] + y1_in[c, 0].astype(F32)).astype(BF16)
            y2_out[c, 0, :, HALF:] = to_up[:, HALF:].astype(BF16)
            to_down = group(slot, down_y)
            y2_out[c, 1, :, :HALF] = to_down[:, :HALF].astype(BF16)
            y2_out[c, 1, :, HALF:] = (to_down[:, HALF:] + y1_in[c, 1].astype(F32)).astype(BF16)
            for copy in y2_copies(c):
                copy.start()

        @pl.when((i >= Y2_LAG) & (i < CHUNKS + Y2_LAG))
        def _():
            c = i - Y2_LAG
            slot = lax.rem(c, ACC_SLOTS)
            for copy in y2_copies(c):
                copy.wait_recv()
            start = pl.multiple_of(c * CHUNK, CHUNK)
            total = group(slot, own_y) + y2_in[c, 0].astype(F32) + y2_in[c, 1].astype(F32)
            total = total.astype(BF16)
            for third in range(3):
                out_ref[jnp.where(lo == 1, 2 - third, third), :, pl.ds(start, CHUNK)] = total[
                    third * UNIT : (third + 1) * UNIT
                ]

        return carry

    lax.fori_loop(0, CHUNKS + Y2_LAG, project_step, 0)

    for copy in gathers:
        copy.wait_send()
    for way in others:
        spread(*way).wait_send()
        deliver(*way).wait_send()

    def drain(c, carry):
        for copy in x_copies(c) + y1_copies(c) + y2_copies(c):
            copy.wait_send()
        return carry

    lax.fori_loop(0, CHUNKS, drain, 0)


def on_device(queries, latent, segments, offsets, w_uk, w_uv, w_out):
    any_spec = pl.BlockSpec(memory_space=pl.ANY)
    smem_spec = pl.BlockSpec(memory_space=pltpu.SMEM)
    dma = pltpu.SemaphoreType.DMA
    out = pl.pallas_call(
        whole_kernel,
        out_shape=jax.ShapeDtypeStruct((3, UNIT, D), BF16),
        in_specs=[smem_spec] * 2 + [any_spec] * 5,
        out_specs=pl.BlockSpec(memory_space=pltpu.VMEM),
        scratch_shapes=[
            pltpu.VMEM((TP, OWN, KV), BF16),
            pltpu.VMEM((ROWS, HEADS * (NOPE + ROPE)), BF16),
            pltpu.VMEM((HEADS, NOPE, LAT), BF16),
            pltpu.VMEM((HEADS, LAT, VH), BF16),
            pltpu.VMEM((ROWS, 2 * ROPE), BF16),
            pltpu.VMEM((ROWS, 2 * ROPE), BF16),
            pltpu.VMEM((NB, BLK, WINDOW * BLK), F32),
            pltpu.VMEM((2, ROWS, 2 * NOPE), BF16),
            pltpu.VMEM((ROWS, 2 * VH), BF16),
            pltpu.VMEM((PAIRS, PARTS, 2, 3, UNIT, PART), BF16),
            pltpu.VMEM((DP, 2, 3, UNIT, PART), BF16),
            pltpu.VMEM((8, 9, UNIT, PART), BF16),
            pltpu.VMEM((8, 3, UNIT, PART), BF16),
            pltpu.VMEM((8, 9, UNIT, PART), BF16),
            pltpu.VMEM((8, 3, UNIT, PART), BF16),
            pltpu.VMEM((12, UNIT, TP * VH), BF16),
            pltpu.VMEM((2, 6, UNIT, TP * VH), BF16),
            pltpu.VMEM((W_SLOTS, TP * VH, CHUNK), BF16),
            pltpu.VMEM((ACC_SLOTS, 12, UNIT, CHUNK), F32),
            pltpu.VMEM((CHUNKS, 2, 2 * OWN, CHUNK), BF16),
            pltpu.VMEM((CHUNKS, 2, 2 * OWN, CHUNK), BF16),
            pltpu.VMEM((CHUNKS, 2, OWN, HALF), BF16),
            pltpu.VMEM((CHUNKS, 2, OWN, HALF), BF16),
            pltpu.VMEM((CHUNKS, 2, OWN, CHUNK), BF16),
            pltpu.VMEM((CHUNKS, 2, OWN, CHUNK), BF16),
            dma((4,)),
            dma((TP - 1,)),
            dma((TP - 1,)),
            dma((DP,)),
            dma((DP,)),
            dma((DP,)),
            dma((DP,)),
            dma((W_SLOTS,)),
        ]
        + [dma((CHUNKS, 2))] * 6,
        compiler_params=pltpu.CompilerParams(
            collective_id=0, has_side_effects=True, vmem_limit_bytes=58 * 2**20
        ),
        name="whole",
    )(segments, offsets, latent, queries, w_uk, w_uv, w_out)
    return out.reshape(OWN, D)


def solution(mesh):
    return jax.shard_map(
        on_device,
        mesh=mesh,
        in_specs=(
            P("dp", "tp"),
            P(("dp", "tp"), None),
            P(),
            P(),
            P("tp", None, None),
            P("tp", None, None),
            P("tp", None),
        ),
        out_specs=P(("dp", "tp"), None),
        check_vma=False,
    )
```

time: 173 us -> 143 us (0.83); the launches traced: 170 us -> 143 us
  Pallas kernels: 160 us -> 139 us
  local copies, waits for them, and re-layouts: 9.44 us -> 3.87 us
    pallas_call x3 -> x1, Pallas kernels: 160 us -> 139 us  [on_device(): pl.pallas_call(whole_kernel, out_shape=jax.ShapeDtypeStruct((3, UNIT, D),...]
    unnamed x14 -> x2, local copies, waits for them, and re-layouts: 9.44 us -> 3.87 us
where the time goes in v2:
time: 143 us
  Pallas kernels  139 us (97%)
  local copies, waits for them, and re-layouts  3.87 us (3%)
    pallas_call x1, Pallas kernels, on_device(): pl.pallas_call(whole_kernel, out_shape=jax.ShapeDtypeStruct((3, UNIT, D),...  139 us
    unnamed x2, local copies, waits for them, and re-layouts  3.87 us

profile of v2, /device:TPU:0, one launch (start us, length us, event | category | flops | bytes accessed | tf_op | source)
XLA Modules:
  0.0 143.0 jit_solution(4408141053323367239)
XLA Ops:
  0.0 1.4 copy.8.seg_ref
  1.4 139.1 %whole.1 = bf16[3,32,7168]{2,1,0:T(8,128)(2,1)} custom-call(s32[16,6]{1,0:T(8,128)} %copy.8.seg_ref, s32[6]{0:T(128)} %off_ref.1, bf16[96,576]{1,0:T(8,128)(2,1)} %lat_hbm.1, bf16[768,1536]{1,0:T(8,128)(2,1)} %q_hbm.1, bf16[8,128,512]{2,1,0:T(8,128)(2,1)} %wuk_hbm.1, bf16[8,512,128]{2,1,0:T(8,128)(2,1)} %wuv_hbm.1, bf16[1024,7168]{1,0:T(8,128)(2,1)} %w_hbm.1), custom_call_target="tpu_custom_call" | custom-call | tf_op jit(solution)/shard_map/whole/pallas_call | solution.py:407
  140.4 2.5 %copy.10 = bf16[96,7168]{1,0:T(8,128)(2,1)} copy(bf16[96,7168]{1,0:T(8,128)(2,1)} %bitcast.1) | data formatting | bytes 2752512

commit v3 on v2

--- a/solution.py
+++ b/solution.py
@@ -31,11 +31,10 @@
 CHUNK = 512
 CHUNKS = D // CHUNK
 HALF = CHUNK // 2
+STEPS = 2 * CHUNKS
 W_SLOTS = 3
-X_LAG = 2
-Y1_LAG = 3
-Y2_LAG = 5
-ACC_SLOTS = Y2_LAG + 1
+GROUPS = (1, 2)
+LAGS = ((3, 4, 6), (2, 3, 5))
 
 MESH = pl.DeviceIdType.MESH
 BF16 = jnp.bfloat16
@@ -70,7 +69,9 @@
     return lax.dot_general(a, b, (((1,), (1,)), ((), ())), preferred_element_type=F32)
 
 
-HOME = ((3, 11, 6), (4, 0, 5), (9, 1, 7), (10, 2, 8))
+HOME = ((11, 3, 6), (4, 0, 5), (7, 1, 9), (2, 10, 8))
+FIRST = (3, 1, 2, 0)
+SECOND = ((2, 4), (0, 3), (1, 6), (7, 5))
 
 
 def unit_of(p, e, u):
@@ -84,12 +85,15 @@
 }
 
 
+def choose(p, options):
+    value = options[0]
+    for i in range(1, PARTS):
+        value = jnp.where(p == i, options[i], value)
+    return value
+
+
 def block_of(p, e, u):
-    first = (
-        jnp.where(p < 2, 1, 4),
-        jnp.where(p == 0, 5, 0),
-        jnp.where(p == 1, 2, 3),
-    )[u]
+    first = choose(p, [unit_of(i, 0, u) // 4 for i in range(PARTS)])
     return jnp.where(e == 1, NB - 1 - first, first)
 
 
@@ -146,8 +150,10 @@
 def whole_kernel(
     seg_ref, off_ref, lat_hbm, q_hbm, wuk_hbm, wuv_hbm, w_hbm, out_ref,
     slab, q_ref, wuk_ref, wuv_ref, rope_even, rope_odd, bias, keys, values,
-    parts, gathered, staged_near, staged_far, near, far, rows_keep, rows_away,
-    w_buf, acc, x_out, x_in, y1_out, y1_in, y2_out, y2_in,
+    parts, gathered, staged_near1, staged_near2, staged_far1, staged_far2, near1, near2, far1, far2,
+    rows1, keep2, away2, w_buf,
+    acc1, x_out1, x_in1, y1_out1, y1_in1, y2_out1, y2_in1,
+    acc2, x_out2, x_in2, y1_out2, y1_in2, y2_out2, y2_in2,
     own_sem, ag_s, ag_r, p1_s, p1_r, p2_s, p2_r,
     w_sem, xs_sem, xr_sem, y1s_sem, y1r_sem, y2s_sem, y2r_sem,
 ):
@@ -168,7 +174,7 @@
         return flip(hi, a) * 8 + lax.rem(z + o, 4) * 2 + flip(core, b)
 
     def load(c):
-        start = pl.multiple_of(c * CHUNK, CHUNK)
+        start = pl.multiple_of(lax.rem(c, CHUNKS) * CHUNK, CHUNK)
         slot = lax.rem(c, W_SLOTS)
         return pltpu.make_async_copy(
             w_hbm.at[:, pl.ds(start, CHUNK)], w_buf.at[slot], w_sem.at[slot]
@@ -191,17 +197,32 @@
         + [(lax.rem(dp + DP // 2, DP), across)]
     )
 
-    gathers = []
-    for o in range(1, TP):
-        copy = remote(
-            lat_hbm, slab.at[tp], ag_s.at[o - 1], ag_r.at[o - 1], dp, lax.rem(tp + o, TP)
-        )
+    opposite = 2 * lax.rem(y + 2, 4) + lo
+    after, before = 2 * lax.rem(y + 1, 4) + lo, 2 * lax.rem(y + 3, 4) + lo
+
+    def hand(index, src, at, to):
+        return remote(src, slab.at[at], ag_s.at[index], ag_r.at[index], dp, to)
+
+    gathers = [
+        hand(0, lat_hbm, tp, opposite),
+        hand(1, lat_hbm, tp, across),
+        hand(2, lat_hbm, tp, after),
+        hand(3, lat_hbm, tp, before),
+        hand(4, slab.at[across], across, after),
+        hand(5, slab.at[across], across, before),
+        hand(6, slab.at[opposite], opposite, across),
+    ]
+    for copy in gathers[:4]:
         copy.start()
-        gathers.append(copy)
+    gathers[1].wait_recv()
+    gathers[4].start()
+    gathers[5].start()
+    gathers[0].wait_recv()
+    gathers[6].start()
     write_bias(seg_ref, bias, dp)
     for copy in loads:
         copy.wait()
-    for copy in gathers:
+    for copy in gathers[2:]:
         copy.wait_recv()
     rope = slab[:, :, LAT:].reshape(ROWS, ROPE)
     blank = jnp.zeros((ROWS, ROPE), BF16)
@@ -244,160 +265,245 @@
     own_part.wait()
 
     part = 2 * core + hi
-    near_sends, far_sends = [], []
+    staged_near, staged_far = (staged_near1, staged_near2), (staged_far1, staged_far2)
+    near, far = (near1, near2), (far1, far2)
 
     def taken(rank, e, u):
         source = lax.rem(rank + DP - off_ref[block_of(part, e, u)], DP)
         return gathered[source, e, u]
 
-    def deliver(o, a, b):
-        at = o * 4 + a * 2 + b
-        src = (staged_far if a else staged_near).at[2 * o + b]
-        dst = (far if a else near).at[2 * z + core]
+    def deliver(g, o, a, b):
+        at = g * DP + o * 4 + a * 2 + b
+        src = (staged_far if a else staged_near)[g].at[2 * o + b]
+        dst = (far if a else near)[g].at[2 * z + core]
         return remote(src, dst, p2_s.at[at], p2_r.at[at], rank_at(o, a, b), tp)
 
-    for o, a, b in ways:
-        rank = rank_at(o, a, b)
-        slot = 2 * o + b
-        if a:
-            target, index = staged_far, slot
-        elif (o, b) == (0, 0):
-            target, index = near, 2 * z + core
-        else:
-            target, index = staged_near, slot
-        for u in range(3):
-            target[index, u] = taken(rank, lo, u)
-        if not a:
-            for side in range(2):
-                for u in range(3):
-                    target[index, 3 + 3 * side + u] = taken(
-                        rank + (side - hi) * 8, 1 - lo, u
-                    )
-        if (o, a, b) != (0, 0, 0):
-            deliver(o, a, b).start()
-    for way in others:
-        deliver(*way).wait_recv()
-
-    for pair in range(PAIRS):
-        columns = pl.ds(pair * PART, PART)
-        for c in range(2):
-            for u in range(3):
-                for a in range(2):
-                    home = jnp.where(hi == 0, HOME[2 * c + a][u], HOME[2 * c + 1 - a][u])
-                    rows_keep[home, :, columns] = (far if a else near)[2 * pair + c, u]
+    for g, units in enumerate(((0,), (1, 2))):
+        for o, a, b in ways:
+            rank = rank_at(o, a, b)
+            own = (o, a, b) == (0, 0, 0)
+            if a:
+                target, index = staged_far[g], 2 * o + b
+            elif own:
+                target, index = near[g], 2 * z + core
+            else:
+                target, index = staged_near[g], 2 * o + b
+            count = len(units)
+            for n, u in enumerate(units):
+                target[index, n] = taken(rank, lo, u)
+            if not a:
                 for side in range(2):
-                    rows_away[side, 3 * c + u, :, columns] = near[2 * pair + c, 3 + 3 * side + u]
-
-    def x_copies(c):
+                    for n, u in enumerate(units):
+                        target[index, count * (1 + side) + n] = taken(
+                            rank + (side - hi) * 8, 1 - lo, u
+                        )
+            if not own:
+                deliver(g, o, a, b).start()
+
+    def arrived(g):
+        for way in others:
+            deliver(g, *way).wait_recv()
+        count = g + 1
+        for pair in range(PAIRS):
+            columns = pl.ds(pair * PART, PART)
+            for c in range(2):
+                for n in range(count):
+                    for a in range(2):
+                        mine, yours = 2 * c + a, 2 * c + 1 - a
+                        unit = (far if a else near)[g][2 * pair + c, n]
+                        if g == 0:
+                            home = jnp.where(hi == 0, FIRST[mine], FIRST[yours])
+                            rows1[4 + home, :, columns] = unit
+                        else:
+                            home = jnp.where(hi == 0, SECOND[mine][n], SECOND[yours][n])
+                            keep2[home, :, columns] = unit
+                    for side in range(2):
+                        unit = near[g][2 * pair + c, count * (1 + side) + n]
+                        if g == 0:
+                            rows1[2 * side + c, :, columns] = unit
+                        else:
+                            away2[side, 2 * c + n, :, columns] = unit
+
+    class Group:
+        pass
+
+    groups = []
+    for g, (acc, x_out, x_in, y1_out, y1_in, y2_out, y2_in) in enumerate(
+        (
+            (acc1, x_out1, x_in1, y1_out1, y1_in1, y2_out1, y2_in1),
+            (acc2, x_out2, x_in2, y1_out2, y1_in2, y2_out2, y2_in2),
+        )
+    ):
+        t = Group()
+        t.acc, t.x_out, t.x_in, t.y1_out, t.y1_in, t.y2_out, t.y2_in = (
+            acc, x_out, x_in, y1_out, y1_in, y2_out, y2_in,
+        )
+        t.g, t.count, t.rows, t.lags = g, GROUPS[g], GROUPS[g] * UNIT, LAGS[g]
+        groups.append(t)
+
+    def x_copies(t, c):
+        sems = t.g * CHUNKS + c
         return [
             remote(
-                x_out.at[c, flip(hi, a)], x_in.at[c, hi], xs_sem.at[c, a], xr_sem.at[c, a],
-                rank_at(0, a, 0), across,
+                t.x_out.at[c, flip(hi, a)], t.x_in.at[c, hi], xs_sem.at[sems, a],
+                xr_sem.at[sems, a], rank_at(0, a, 0), across,
             )
             for a in range(2)
         ]
 
-    def y1_copies(c):
+    def y_copies(t, c, out, into, send, recv):
+        sems = t.g * CHUNKS + c
         return [
-            remote(y1_out.at[c, 0], y1_in.at[c, 0], y1s_sem.at[c, 0], y1r_sem.at[c, 0], dp, up),
-            remote(y1_out.at[c, 1], y1_in.at[c, 1], y1s_sem.at[c, 1], y1r_sem.at[c, 1], dp, down),
+            remote(out.at[c, a], into.at[c, a], send.at[sems, a], recv.at[sems, a], dp, to)
+            for a, to in enumerate((up, down))
         ]
 
-    def y2_copies(c):
-        return [
-            remote(y2_out.at[c, 0], y2_in.at[c, 0], y2s_sem.at[c, 0], y2r_sem.at[c, 0], dp, up),
-            remote(y2_out.at[c, 1], y2_in.at[c, 1], y2s_sem.at[c, 1], y2r_sem.at[c, 1], dp, down),
-        ]
-
-    def group(slot, at):
-        return acc[slot, pl.ds(3 * at, 3)].reshape(OWN, CHUNK)
-
-    def project_step(i, carry):
-        @pl.when(i < CHUNKS)
+    def y1_copies(t, c):
+        return y_copies(t, c, t.y1_out, t.y1_in, y1s_sem, y1r_sem)
+
+    def y2_copies(t, c):
+        return y_copies(t, c, t.y2_out, t.y2_in, y2s_sem, y2r_sem)
+
+    def sums(t, slot, at):
+        return t.acc[slot, pl.ds(t.count * at, t.count)].reshape(t.rows, CHUNK)
+
+    def multiply(t, i):
+        c = i - t.g * CHUNKS
+        slot = lax.rem(i, W_SLOTS)
+        load(i).wait()
+
+        @pl.when(i + W_SLOTS - 1 < STEPS)
         def _():
-            slot = lax.rem(i, W_SLOTS)
-            load(i).wait()
-
-            @pl.when(i + W_SLOTS - 1 < CHUNKS)
-            def _():
-                load(i + W_SLOTS - 1).start()
-
-            w = w_buf[slot]
-            x_out[i] = (
-                jnp.dot(rows_away[...].reshape(4 * OWN, TP * VH), w, preferred_element_type=F32)
+            load(i + W_SLOTS - 1).start()
+
+        w = w_buf[slot]
+        at = lax.rem(c, t.lags[2] + 1)
+        if t.g == 0:
+            both = jnp.dot(
+                rows1[...].reshape(8 * UNIT, TP * VH), w, preferred_element_type=F32
+            )
+            t.x_out[c] = both[: 4 * UNIT].astype(BF16).reshape(2, 2 * UNIT, CHUNK)
+            for copy in x_copies(t, c):
+                copy.start()
+            t.acc[at] = both[4 * UNIT :].reshape(4, UNIT, CHUNK)
+        else:
+            t.x_out[c] = (
+                jnp.dot(away2[...].reshape(8 * UNIT, TP * VH), w, preferred_element_type=F32)
                 .astype(BF16)
-                .reshape(2, 2 * OWN, CHUNK)
+                .reshape(2, 4 * UNIT, CHUNK)
             )
-            for copy in x_copies(i):
+            for copy in x_copies(t, c):
                 copy.start()
-            acc[lax.rem(i, ACC_SLOTS)] = jnp.dot(
-                rows_keep[...].reshape(4 * OWN, TP * VH), w, preferred_element_type=F32
-            ).reshape(12, UNIT, CHUNK)
-
-        @pl.when((i >= X_LAG) & (i < CHUNKS + X_LAG))
-        def _():
-            c = i - X_LAG
-            slot = lax.rem(c, ACC_SLOTS)
-            for copy in x_copies(c):
-                copy.wait_recv()
-            for side in range(2):
-                for half in range(2):
-                    for u in range(3):
-                        home = HOME[2 * half + side][u]
-                        acc[slot, home] = acc[slot, home] + x_in[
-                            c, side, pl.ds((3 * half + u) * UNIT, UNIT)
-                        ].astype(F32)
-            other = group(slot, far_y).astype(BF16)
-            y1_out[c, 0] = other[:, :HALF]
-            y1_out[c, 1] = other[:, HALF:]
-            for copy in y1_copies(c):
-                copy.start()
-
-        @pl.when((i >= Y1_LAG) & (i < CHUNKS + Y1_LAG))
-        def _():
-            c = i - Y1_LAG
-            slot = lax.rem(c, ACC_SLOTS)
-            for copy in y1_copies(c):
-                copy.wait_recv()
-            to_up = group(slot, up_y)
-            y2_out[c, 0, :, :HALF] = (to_up[:, :HALF] + y1_in[c, 0].astype(F32)).astype(BF16)
-            y2_out[c, 0, :, HALF:] = to_up[:, HALF:].astype(BF16)
-            to_down = group(slot, down_y)
-            y2_out[c, 1, :, :HALF] = to_down[:, :HALF].astype(BF16)
-            y2_out[c, 1, :, HALF:] = (to_down[:, HALF:] + y1_in[c, 1].astype(F32)).astype(BF16)
-            for copy in y2_copies(c):
-                copy.start()
-
-        @pl.when((i >= Y2_LAG) & (i < CHUNKS + Y2_LAG))
-        def _():
-            c = i - Y2_LAG
-            slot = lax.rem(c, ACC_SLOTS)
-            for copy in y2_copies(c):
-                copy.wait_recv()
-            start = pl.multiple_of(c * CHUNK, CHUNK)
-            total = group(slot, own_y) + y2_in[c, 0].astype(F32) + y2_in[c, 1].astype(F32)
-            total = total.astype(BF16)
-            for third in range(3):
-                out_ref[jnp.where(lo == 1, 2 - third, third), :, pl.ds(start, CHUNK)] = total[
-                    third * UNIT : (third + 1) * UNIT
-                ]
-
+            t.acc[at] = jnp.dot(
+                keep2[...].reshape(8 * UNIT, TP * VH), w, preferred_element_type=F32
+            ).reshape(8, UNIT, CHUNK)
+
+    def after_x(t, c):
+        slot = lax.rem(c, t.lags[2] + 1)
+        for copy in x_copies(t, c):
+            copy.wait_recv()
+        for side in range(2):
+            for half in range(2):
+                for n in range(t.count):
+                    p = 2 * half + side
+                    home = SECOND[p][n] if t.g else FIRST[p]
+                    t.acc[slot, home] = t.acc[slot, home] + t.x_in[
+                        c, side, pl.ds((t.count * half + n) * UNIT, UNIT)
+                    ].astype(F32)
+        other = sums(t, slot, far_y).astype(BF16)
+        t.y1_out[c, 0] = other[:, :HALF]
+        t.y1_out[c, 1] = other[:, HALF:]
+        for copy in y1_copies(t, c):
+            copy.start()
+
+    def after_y1(t, c):
+        slot = lax.rem(c, t.lags[2] + 1)
+        for copy in y1_copies(t, c):
+            copy.wait_recv()
+        to_up = sums(t, slot, up_y)
+        t.y2_out[c, 0, :, :HALF] = (to_up[:, :HALF] + t.y1_in[c, 0].astype(F32)).astype(BF16)
+        t.y2_out[c, 0, :, HALF:] = to_up[:, HALF:].astype(BF16)
+        to_down = sums(t, slot, down_y)
+        t.y2_out[c, 1, :, :HALF] = to_down[:, :HALF].astype(BF16)
+        t.y2_out[c, 1, :, HALF:] = (to_down[:, HALF:] + t.y1_in[c, 1].astype(F32)).astype(BF16)
+        for copy in y2_copies(t, c):
+            copy.start()
+
+    edge = (own_y == 0) | (own_y == 3)
+
+    def after_y2(t, c):
+        slot = lax.rem(c, t.lags[2] + 1)
+        for copy in y2_copies(t, c):
+            copy.wait_recv()
+        start = pl.multiple_of(c * CHUNK, CHUNK)
+        total = sums(t, slot, own_y) + t.y2_in[c, 0].astype(F32) + t.y2_in[c, 1].astype(F32)
+        total = total.astype(BF16)
+        if t.g == 0:
+            thirds = [jnp.where(edge, 2, 1)]
+        else:
+            thirds = [0, jnp.where(edge, 1, 2)]
+        for n, third in enumerate(thirds):
+            out_ref[jnp.where(lo == 1, 2 - third, third), :, pl.ds(start, CHUNK)] = total[
+                n * UNIT : (n + 1) * UNIT
+            ]
+
+    def later(t, i, least, most):
+        for lag, stage in zip(t.lags, (after_x, after_y1, after_y2)):
+            low = t.g * CHUNKS + lag
+            if most > low and least < low + CHUNKS:
+
+                @pl.when((i >= low) & (i < low + CHUNKS))
+                def _(stage=stage, low=low):
+                    stage(t, i - low)
+
+    def first_step(i, carry):
+        multiply(groups[0], i)
+        later(groups[0], i, 0, CHUNKS)
         return carry
 
-    lax.fori_loop(0, CHUNKS + Y2_LAG, project_step, 0)
+    def second_step(i, carry):
+        multiply(groups[1], i)
+        later(groups[0], i, CHUNKS, STEPS)
+        later(groups[1], i, CHUNKS, STEPS)
+        return carry
+
+    def last_step(i, carry):
+        later(groups[1], i, STEPS, STEPS + LAGS[1][2])
+        return carry
+
+    arrived(0)
+    lax.fori_loop(0, CHUNKS, first_step, 0)
+    arrived(1)
+    lax.fori_loop(CHUNKS, STEPS, second_step, 0)
+    lax.fori_loop(STEPS, STEPS + LAGS[1][2], last_step, 0)
 
     for copy in gathers:
         copy.wait_send()
     for way in others:
         spread(*way).wait_send()
-        deliver(*way).wait_send()
+        deliver(0, *way).wait_send()
+        deliver(1, *way).wait_send()
 
     def drain(c, carry):
-        for copy in x_copies(c) + y1_copies(c) + y2_copies(c):
-            copy.wait_send()
+        for t in groups:
+            for copy in x_copies(t, c) + y1_copies(t, c) + y2_copies(t, c):
+                copy.wait_send()
         return carry
 
     lax.fori_loop(0, CHUNKS, drain, 0)
+
+
+def sum_scratch(g):
+    rows = GROUPS[g] * UNIT
+    return [
+        pltpu.VMEM((LAGS[g][2] + 1, 4 * GROUPS[g], UNIT, CHUNK), F32),
+        pltpu.VMEM((CHUNKS, 2, 2 * rows, CHUNK), BF16),
+        pltpu.VMEM((CHUNKS, 2, 2 * rows, CHUNK), BF16),
+        pltpu.VMEM((CHUNKS, 2, rows, HALF), BF16),
+        pltpu.VMEM((CHUNKS, 2, rows, HALF), BF16),
+        pltpu.VMEM((CHUNKS, 2, rows, CHUNK), BF16),
+        pltpu.VMEM((CHUNKS, 2, rows, CHUNK), BF16),
+    ]
 
 
 def on_device(queries, latent, segments, offsets, w_uk, w_uv, w_out):
@@ -421,30 +527,32 @@
             pltpu.VMEM((ROWS, 2 * VH), BF16),
             pltpu.VMEM((PAIRS, PARTS, 2, 3, UNIT, PART), BF16),
             pltpu.VMEM((DP, 2, 3, UNIT, PART), BF16),
-            pltpu.VMEM((8, 9, UNIT, PART), BF16),
             pltpu.VMEM((8, 3, UNIT, PART), BF16),
-            pltpu.VMEM((8, 9, UNIT, PART), BF16),
+            pltpu.VMEM((8, 6, UNIT, PART), BF16),
+            pltpu.VMEM((8, 1, UNIT, PART), BF16),
+            pltpu.VMEM((8, 2, UNIT, PART), BF16),
             pltpu.VMEM((8, 3, UNIT, PART), BF16),
-            pltpu.VMEM((12, UNIT, TP * VH), BF16),
-            pltpu.VMEM((2, 6, UNIT, TP * VH), BF16),
+            pltpu.VMEM((8, 6, UNIT, PART), BF16),
+            pltpu.VMEM((8, 1, UNIT, PART), BF16),
+            pltpu.VMEM((8, 2, UNIT, PART), BF16),
+            pltpu.VMEM((8, UNIT, TP * VH), BF16),
+            pltpu.VMEM((8, UNIT, TP * VH), BF16),
+            pltpu.VMEM((2, 4, UNIT, TP * VH), BF16),
             pltpu.VMEM((W_SLOTS, TP * VH, CHUNK), BF16),
-            pltpu.VMEM((ACC_SLOTS, 12, UNIT, CHUNK), F32),
-            pltpu.VMEM((CHUNKS, 2, 2 * OWN, CHUNK), BF16),
-            pltpu.VMEM((CHUNKS, 2, 2 * OWN, CHUNK), BF16),
-            pltpu.VMEM((CHUNKS, 2, OWN, HALF), BF16),
-            pltpu.VMEM((CHUNKS, 2, OWN, HALF), BF16),
-            pltpu.VMEM((CHUNKS, 2, OWN, CHUNK), BF16),
-            pltpu.VMEM((CHUNKS, 2, OWN, CHUNK), BF16),
+        ]
+        + sum_scratch(0)
+        + sum_scratch(1)
+        + [
             dma((4,)),
             dma((TP - 1,)),
             dma((TP - 1,)),
             dma((DP,)),
             dma((DP,)),
-            dma((DP,)),
-            dma((DP,)),
+            dma((2 * DP,)),
+            dma((2 * DP,)),
             dma((W_SLOTS,)),
         ]
-        + [dma((CHUNKS, 2))] * 6,
+        + [dma((STEPS, 2))] * 6,
         compiler_params=pltpu.CompilerParams(
             collective_id=0, has_side_effects=True, vmem_limit_bytes=58 * 2**20
         ),

time: 143 us -> 139 us (0.972)
  Pallas kernels: 139 us -> 135 us
    pallas_call x1, Pallas kernels: 139 us -> 135 us  [on_device(): pl.pallas_call(whole_kernel, out_shape=jax.ShapeDtypeStruct((3, UNIT, D),...]
where the time goes in v3:
time: 139 us
  Pallas kernels  135 us (97%)
  local copies, waits for them, and re-layouts  3.87 us (3%)
    pallas_call x1, Pallas kernels, on_device(): pl.pallas_call(whole_kernel, out_shape=jax.ShapeDtypeStruct((3, UNIT, D),...  135 us
    unnamed x2, local copies, waits for them, and re-layouts  3.87 us

profile of v3, /device:TPU:0, one launch (start us, length us, event | category | flops | bytes accessed | tf_op | source)
XLA Modules:
  0.0 138.9 jit_solution(17628685056572193451)
XLA Ops:
  0.0 1.4 copy.8.seg_ref
  1.4 135.0 %whole.1 = bf16[3,32,7168]{2,1,0:T(8,128)(2,1)} custom-call(s32[16,6]{1,0:T(8,128)} %copy.8.seg_ref, s32[6]{0:T(128)} %off_ref.1, bf16[96,576]{1,0:T(8,128)(2,1)} %lat_hbm.1, bf16[768,1536]{1,0:T(8,128)(2,1)} %q_hbm.1, bf16[8,128,512]{2,1,0:T(8,128)(2,1)} %wuk_hbm.1, bf16[8,512,128]{2,1,0:T(8,128)(2,1)} %wuv_hbm.1, bf16[1024,7168]{1,0:T(8,128)(2,1)} %w_hbm.1), custom_call_target="tpu_custom_call" | custom-call | tf_op jit(solution)/shard_map/whole/pallas_call | solution.py:513
  136.4 2.5 %copy.10 = bf16[96,7168]{1,0:T(8,128)(2,1)} copy(bf16[96,7168]{1,0:T(8,128)(2,1)} %bitcast.1) | data formatting | bytes 2752512

commit v4 on v3

--- a/solution.py
+++ b/solution.py
@@ -34,7 +34,8 @@
 STEPS = 2 * CHUNKS
 W_SLOTS = 3
 GROUPS = (1, 2)
-LAGS = ((3, 4, 6), (2, 3, 5))
+LAGS = ((4, 7, 10), (3, 5, 8))
+Y_FIRST = 6
 
 MESH = pl.DeviceIdType.MESH
 BF16 = jnp.bfloat16
@@ -72,6 +73,7 @@
 HOME = ((11, 3, 6), (4, 0, 5), (7, 1, 9), (2, 10, 8))
 FIRST = (3, 1, 2, 0)
 SECOND = ((2, 4), (0, 3), (1, 6), (7, 5))
+AWAY = ((2, 0, 1, 3), (0, 1, 3, 2))
 
 
 def unit_of(p, e, u):
@@ -154,8 +156,10 @@
     rows1, keep2, away2, w_buf,
     acc1, x_out1, x_in1, y1_out1, y1_in1, y2_out1, y2_in1,
     acc2, x_out2, x_in2, y1_out2, y1_in2, y2_out2, y2_in2,
+    a1_out, a1_in, a2_out, a2_in, x2_out, x2_in,
     own_sem, ag_s, ag_r, p1_s, p1_r, p2_s, p2_r,
     w_sem, xs_sem, xr_sem, y1s_sem, y1r_sem, y2s_sem, y2r_sem,
+    a1s_sem, a1r_sem, a2s_sem, a2r_sem, x2s_sem, x2r_sem,
 ):
     dp, tp = ranks()
     y, lo = tp // 2, lax.rem(tp, 2)
@@ -382,7 +386,7 @@
             both = jnp.dot(
                 rows1[...].reshape(8 * UNIT, TP * VH), w, preferred_element_type=F32
             )
-            t.x_out[c] = both[: 4 * UNIT].astype(BF16).reshape(2, 2 * UNIT, CHUNK)
+            t.x_out[c] = both[: 4 * UNIT].astype(BF16).reshape(2, 2, UNIT, CHUNK)
             for copy in x_copies(t, c):
                 copy.start()
             t.acc[at] = both[4 * UNIT :].reshape(4, UNIT, CHUNK)
@@ -390,15 +394,75 @@
             t.x_out[c] = (
                 jnp.dot(away2[...].reshape(8 * UNIT, TP * VH), w, preferred_element_type=F32)
                 .astype(BF16)
-                .reshape(2, 4 * UNIT, CHUNK)
+                .reshape(2, 4, UNIT, CHUNK)
             )
-            for copy in x_copies(t, c):
-                copy.start()
+            start_x(t, c)
+            start_y_first(t, c)
             t.acc[at] = jnp.dot(
                 keep2[...].reshape(8 * UNIT, TP * VH), w, preferred_element_type=F32
             ).reshape(8, UNIT, CHUNK)
 
-    def after_x(t, c):
+    def goes_over_x(t, c, to):
+        return (c >= Y_FIRST) | (lax.rem(c, 2) != to)
+
+    def start_x(t, c):
+        for a, copy in enumerate(x_copies(t, c)):
+            pl.when(goes_over_x(t, c, flip(hi, a)))(copy.start)
+
+    def away_unit(c, to):
+        at = choose(3 - to, [jnp.where(hi == 0, AWAY[0][i], AWAY[1][i]) for i in range(4)])
+        return x_out2[c, lax.rem(c, 2), at]
+
+    def a1_copies(c):
+        return [
+            remote(a1_out.at[c, a], a1_in.at[c, a], a1s_sem.at[c, a], a1r_sem.at[c, a], dp, to)
+            for a, to in enumerate((up, down))
+        ]
+
+    def a2_copies(c):
+        return [
+            remote(a2_out.at[c, a], a2_in.at[c, a], a2s_sem.at[c, a], a2r_sem.at[c, a], dp, to)
+            for a, to in enumerate((up, down))
+        ]
+
+    def x2_copy(c):
+        rank = lax.rem(c, 2) * 8 + 2 * z + core
+        return remote(x2_out.at[c], x2_in.at[c, hi], x2s_sem.at[c], x2r_sem.at[c, hi], rank, across)
+
+    def start_y_first(t, c):
+        @pl.when(c < Y_FIRST)
+        def _():
+            other = away_unit(c, far_y)
+            a1_out[c, 0] = other[:, :HALF]
+            a1_out[c, 1] = other[:, HALF:]
+            for copy in a1_copies(c):
+                copy.start()
+
+    def after_a1(t, c):
+        for copy in a1_copies(c):
+            copy.wait_recv()
+        to_up = away_unit(c, up_y)
+        a2_out[c, 0, :, :HALF] = (
+            to_up[:, :HALF].astype(F32) + a1_in[c, 0].astype(F32)
+        ).astype(BF16)
+        a2_out[c, 0, :, HALF:] = to_up[:, HALF:]
+        to_down = away_unit(c, down_y)
+        a2_out[c, 1, :, :HALF] = to_down[:, :HALF]
+        a2_out[c, 1, :, HALF:] = (
+            to_down[:, HALF:].astype(F32) + a1_in[c, 1].astype(F32)
+        ).astype(BF16)
+        for copy in a2_copies(c):
+            copy.start()
+
+    def after_a2(t, c):
+        for copy in a2_copies(c):
+            copy.wait_recv()
+        x2_out[c] = (
+            away_unit(c, own_y).astype(F32) + a2_in[c, 0].astype(F32) + a2_in[c, 1].astype(F32)
+        ).astype(BF16)
+        x2_copy(c).start()
+
+    def add_x(t, c):
         slot = lax.rem(c, t.lags[2] + 1)
         for copy in x_copies(t, c):
             copy.wait_recv()
@@ -408,8 +472,15 @@
                     p = 2 * half + side
                     home = SECOND[p][n] if t.g else FIRST[p]
                     t.acc[slot, home] = t.acc[slot, home] + t.x_in[
-                        c, side, pl.ds((t.count * half + n) * UNIT, UNIT)
+                        c, side, t.count * half + n
                     ].astype(F32)
+
+    def after_x(t, c):
+        if t.g == 0:
+            add_x(t, c)
+        else:
+            pl.when(goes_over_x(t, c, hi))(lambda: add_x(t, c))
+        slot = lax.rem(c, t.lags[2] + 1)
         other = sums(t, slot, far_y).astype(BF16)
         t.y1_out[c, 0] = other[:, :HALF]
         t.y1_out[c, 1] = other[:, HALF:]
@@ -436,16 +507,36 @@
         for copy in y2_copies(t, c):
             copy.wait_recv()
         start = pl.multiple_of(c * CHUNK, CHUNK)
-        total = sums(t, slot, own_y) + t.y2_in[c, 0].astype(F32) + t.y2_in[c, 1].astype(F32)
-        total = total.astype(BF16)
         if t.g == 0:
             thirds = [jnp.where(edge, 2, 1)]
         else:
             thirds = [0, jnp.where(edge, 1, 2)]
-        for n, third in enumerate(thirds):
-            out_ref[jnp.where(lo == 1, 2 - third, third), :, pl.ds(start, CHUNK)] = total[
-                n * UNIT : (n + 1) * UNIT
-            ]
+
+        def finish(more):
+            total = sums(t, slot, own_y) + t.y2_in[c, 0].astype(F32) + t.y2_in[c, 1].astype(F32)
+            for n, third in enumerate(thirds):
+                unit = total[n * UNIT : (n + 1) * UNIT]
+                if more:
+                    side = jnp.where(own_y == 0, 1 - n, n)
+                    unit = unit + x2_in[c, side].astype(F32)
+                out_ref[jnp.where(lo == 1, 2 - third, third), :, pl.ds(start, CHUNK)] = (
+                    unit.astype(BF16)
+                )
+
+        if t.g == 0:
+            finish(False)
+        else:
+            over_x = goes_over_x(t, c, hi)
+            pl.when(over_x)(lambda: finish(False))
+
+            @pl.when(jnp.logical_not(over_x))
+            def _():
+                for side in range(2):
+                    remote(
+                        x2_out.at[c], x2_in.at[c, side], x2s_sem.at[c], x2r_sem.at[c, side],
+                        dp, across,
+                    ).wait_recv()
+                finish(True)
 
     def later(t, i, least, most):
         for lag, stage in zip(t.lags, (after_x, after_y1, after_y2)):
@@ -453,6 +544,14 @@
             if most > low and least < low + CHUNKS:
 
                 @pl.when((i >= low) & (i < low + CHUNKS))
+                def _(stage=stage, low=low):
+                    stage(t, i - low)
+
+        if t.g == 1:
+            for lag, stage in zip(t.lags[:2], (after_a1, after_a2)):
+                low = CHUNKS + lag
+
+                @pl.when((i >= low) & (i < low + Y_FIRST))
                 def _(stage=stage, low=low):
                     stage(t, i - low)
 
@@ -486,8 +585,18 @@
 
     def drain(c, carry):
         for t in groups:
-            for copy in x_copies(t, c) + y1_copies(t, c) + y2_copies(t, c):
+            for copy in y1_copies(t, c) + y2_copies(t, c):
                 copy.wait_send()
+        for copy in x_copies(groups[0], c):
+            copy.wait_send()
+        for a, copy in enumerate(x_copies(groups[1], c)):
+            pl.when(goes_over_x(groups[1], c, flip(hi, a)))(copy.wait_send)
+
+        @pl.when(c < Y_FIRST)
+        def _():
+            for copy in a1_copies(c) + a2_copies(c) + [x2_copy(c)]:
+                copy.wait_send()
+
         return carry
 
     lax.fori_loop(0, CHUNKS, drain, 0)
@@ -497,8 +606,8 @@
     rows = GROUPS[g] * UNIT
     return [
         pltpu.VMEM((LAGS[g][2] + 1, 4 * GROUPS[g], UNIT, CHUNK), F32),
-        pltpu.VMEM((CHUNKS, 2, 2 * rows, CHUNK), BF16),
-        pltpu.VMEM((CHUNKS, 2, 2 * rows, CHUNK), BF16),
+        pltpu.VMEM((CHUNKS, 2, 2 * GROUPS[g], UNIT, CHUNK), BF16),
+        pltpu.VMEM((CHUNKS, 2, 2 * GROUPS[g], UNIT, CHUNK), BF16),
         pltpu.VMEM((CHUNKS, 2, rows, HALF), BF16),
         pltpu.VMEM((CHUNKS, 2, rows, HALF), BF16),
         pltpu.VMEM((CHUNKS, 2, rows, CHUNK), BF16),
@@ -543,6 +652,12 @@
         + sum_scratch(0)
         + sum_scratch(1)
         + [
+            pltpu.VMEM((Y_FIRST, 2, UNIT, HALF), BF16),
+            pltpu.VMEM((Y_FIRST, 2, UNIT, HALF), BF16),
+            pltpu.VMEM((Y_FIRST, 2, UNIT, CHUNK), BF16),
+            pltpu.VMEM((Y_FIRST, 2, UNIT, CHUNK), BF16),
+            pltpu.VMEM((Y_FIRST, UNIT, CHUNK), BF16),
+            pltpu.VMEM((Y_FIRST, 2, UNIT, CHUNK), BF16),
             dma((4,)),
             dma((TP - 1,)),
             dma((TP - 1,)),
@@ -552,7 +667,9 @@
             dma((2 * DP,)),
             dma((W_SLOTS,)),
         ]
-        + [dma((STEPS, 2))] * 6,
+        + [dma((STEPS, 2))] * 6
+        + [dma((Y_FIRST, 2))] * 4
+        + [dma((Y_FIRST,)), dma((Y_FIRST, 2))],
         compiler_params=pltpu.CompilerParams(
             collective_id=0, has_side_effects=True, vmem_limit_bytes=58 * 2**20
         ),

time: 139 us -> 130 us (0.935)
  Pallas kernels: 135 us -> 126 us
    pallas_call x1, Pallas kernels: 135 us -> 126 us  [on_device(): pl.pallas_call(whole_kernel, out_shape=jax.ShapeDtypeStruct((3, UNIT, D),...]
where the time goes in v4:
time: 130 us
  Pallas kernels  126 us (97%)
  local copies, waits for them, and re-layouts  3.87 us (3%)
    pallas_call x1, Pallas kernels, on_device(): pl.pallas_call(whole_kernel, out_shape=jax.ShapeDtypeStruct((3, UNIT, D),...  126 us
    unnamed x2, local copies, waits for them, and re-layouts  3.87 us

profile of v4, /device:TPU:0, one launch (start us, length us, event | category | flops | bytes accessed | tf_op | source)
XLA Modules:
  0.0 129.7 jit_solution(4033759456463465193)
XLA Ops:
  0.0 1.4 %copy.8.seg_ref = s32[16,6]{1,0:T(8,128)} copy(s32[16,6]{0,1:T(8,128)} %param.9) | data formatting | bytes 768 | tf_op args[2]
  1.4 125.8 %whole.1 = bf16[3,32,7168]{2,1,0:T(8,128)(2,1)} custom-call(s32[16,6]{1,0:T(8,128)} %copy.8.seg_ref, s32[6]{0:T(128)} %off_ref.1, bf16[96,576]{1,0:T(8,128)(2,1)} %lat_hbm.1, bf16[768,1536]{1,0:T(8,128)(2,1)} %q_hbm.1, bf16[8,128,512]{2,1,0:T(8,128)(2,1)} %wuk_hbm.1, bf16[8,512,128]{2,1,0:T(8,128)(2,1)} %wuv_hbm.1, bf16[1024,7168]{1,0:T(8,128)(2,1)} %w_hbm.1), custom_call_target="tpu_custom_call" | custom-call | tf_op jit(solution)/shard_map/whole/pallas_call | solution.py:622
  127.2 2.5 %copy.10 = bf16[96,7168]{1,0:T(8,128)(2,1)} copy(bf16[96,7168]{1,0:T(8,128)(2,1)} %bitcast.1) | data formatting | bytes 2752512

commit v5 on v4

--- a/solution.py
+++ b/solution.py
@@ -35,7 +35,9 @@
 W_SLOTS = 3
 GROUPS = (1, 2)
 LAGS = ((4, 7, 10), (3, 5, 8))
-Y_FIRST = 6
+Y_FIRST = 5
+AHEAD = 3
+DELIVER_AT = 5
 
 MESH = pl.DeviceIdType.MESH
 BF16 = jnp.bfloat16
@@ -87,6 +89,21 @@
 }
 
 
+HOLDS = (
+    tuple(((FIRST.index(y) % 2, FIRST.index(y) // 2),) for y in range(4)),
+    tuple(
+        tuple(
+            (p % 2, 2 * (p // 2) + n)
+            for home in (2 * y, 2 * y + 1)
+            for p in range(PARTS)
+            for n in range(2)
+            if SECOND[p][n] == home
+        )
+        for y in range(4)
+    ),
+)
+
+
 def choose(p, options):
     value = options[0]
     for i in range(1, PARTS):
@@ -108,12 +125,12 @@
             if kb == qb:
                 block = jnp.where(col <= row, 0.0, -jnp.inf).astype(F32)
             else:
-                same = seg_ref[dp, kb] == seg_ref[dp, qb]
+                same = seg_ref[kb, dp] == seg_ref[qb, dp]
                 block = jnp.full((BLK, BLK), jnp.where(same, 0.0, -jnp.inf), F32)
             bias[qb, :, (kb - first) * BLK : (kb - first + 1) * BLK] = block
 
 
-def attend_pair(pair, slab, rope_even, rope_odd, bias, q_ref, wuk_ref, wuv_ref, keys, values, parts):
+def attend_pair(pair, slab, rope_even, rope_odd, bias, q_ref, wuk_ref, wuv_ref, keys, values, parts1, parts2):
     content = slab[:, :, :LAT].reshape(ROWS, LAT)
     up = wuk_ref[pl.ds(2 * pair, 2)].reshape(2 * NOPE, LAT)
     both = nt_dot(content, up)
@@ -124,35 +141,47 @@
     keys[1, :, :NOPE] = jnp.where(lane < 64, 0.0, turned).astype(BF16)
     keys[1, :, NOPE:] = jnp.where(lane < 64, turned, rope_odd[...].astype(F32)).astype(BF16)
     for e in range(2):
-        values[:, e * VH : (e + 1) * VH] = jnp.dot(
+        values[e, :, :VH] = jnp.dot(
             content, wuv_ref[2 * pair + e], preferred_element_type=F32
         ).astype(BF16)
-    for qb in range(NB):
+
+    def window(qb):
         first = max(0, qb - WINDOW + 1)
-        keep = pl.ds(first * BLK, (qb - first + 1) * BLK)
-        for e in range(2):
-            start = pl.multiple_of(pair * 384 + 128 * e, 128)
-            q = q_ref[pl.ds(qb * BLK, BLK), pl.ds(start, 256)]
-            s = nt_dot(q, keys[e, keep, :])
-            s = s + bias[qb, :, : (qb - first + 1) * BLK]
-            top = jnp.max(s, axis=1, keepdims=True)
-            p = jnp.exp2((s - top) * (SCALE * LOG2E))
-            total = jnp.sum(p, axis=1, keepdims=True)
-            o = jnp.dot(
-                p.astype(BF16), values[keep, e * VH : (e + 1) * VH], preferred_element_type=F32
-            )
-            o = (o / total).astype(BF16)
-            for quarter in range(4):
-                part, side, u = PLACE[4 * qb + quarter]
-                parts[pair, part, side, u, :, e * VH : (e + 1) * VH] = o[
-                    quarter * UNIT : (quarter + 1) * UNIT
-                ]
+        return pl.ds(first * BLK, (qb - first + 1) * BLK), (qb - first + 1) * BLK
+
+    def score(qb, e):
+        keep, width = window(qb)
+        start = pl.multiple_of(pair * 384 + 128 * e, 128)
+        q = q_ref[pl.ds(qb * BLK, BLK), pl.ds(start, 256)]
+        return nt_dot(q, keys[e, keep, :]) + bias[qb, :, :width]
+
+    def finish(qb, e, s):
+        keep, _ = window(qb)
+        top = jnp.max(s, axis=1, keepdims=True)
+        p = jnp.exp2((s - top) * (SCALE * LOG2E)).astype(BF16)
+        o = jnp.dot(p, values[e, keep, :], preferred_element_type=F32)
+        o = (o[:, :VH] / o[:, VH:]).astype(BF16)
+        for quarter in range(4):
+            part, side, u = PLACE[4 * qb + quarter]
+            target, n = (parts2, u - 1) if u else (parts1, 0)
+            target[pair, part, side, n, :, e * VH : (e + 1) * VH] = o[
+                quarter * UNIT : (quarter + 1) * UNIT
+            ]
+
+    units = [(qb, e) for qb in range(NB) for e in range(2)]
+    waiting = []
+    for unit in units:
+        waiting.append((*unit, score(*unit)))
+        if len(waiting) > AHEAD:
+            finish(*waiting.pop(0))
+    for held in waiting:
+        finish(*held)
 
 
 def whole_kernel(
     seg_ref, off_ref, lat_hbm, q_hbm, wuk_hbm, wuv_hbm, w_hbm, out_ref,
     slab, q_ref, wuk_ref, wuv_ref, rope_even, rope_odd, bias, keys, values,
-    parts, gathered, staged_near1, staged_near2, staged_far1, staged_far2, near1, near2, far1, far2,
+    parts1, parts2, gathered1, gathered2, staged_near1, staged_near2, staged_far1, staged_far2, near1, near2, far1, far2,
     rows1, keep2, away2, w_buf,
     acc1, x_out1, x_in1, y1_out1, y1_in1, y2_out1, y2_in1,
     acc2, x_out2, x_in2, y1_out2, y1_in2, y2_out2, y2_in2,
@@ -232,41 +261,57 @@
     blank = jnp.zeros((ROWS, ROPE), BF16)
     rope_even[...] = jnp.concatenate([rope, blank], axis=1)
     rope_odd[...] = jnp.concatenate([blank, rope], axis=1)
-
-    def spread(o, a, b):
+    values[:, :, VH:] = jnp.ones((2, ROWS, VH), BF16)
+
+    parts, gathered = (parts1, parts2), (gathered1, gathered2)
+
+    def spread(g, o, a, b):
         pair = lax.rem(z + o, 4)
         part = 2 * flip(core, b) + flip(hi, a)
-        at = o * 4 + a * 2 + b
+        at = g * DP + o * 4 + a * 2 + b
         return remote(
-            parts.at[pair, part], gathered.at[dp], p1_s.at[at], p1_r.at[at], rank_at(o, a, b), tp
+            parts[g].at[pair, part], gathered[g].at[dp], p1_s.at[at], p1_r.at[at],
+            rank_at(o, a, b), tp,
         )
 
-    own_part = pltpu.make_async_copy(
-        parts.at[z, 2 * core + hi], gathered.at[dp], p1_s.at[0]
-    )
+    def own_part(g):
+        return pltpu.make_async_copy(
+            parts[g].at[z, 2 * core + hi], gathered[g].at[dp], p1_s.at[g * DP]
+        )
 
     def attend_step(i, carry):
         o = jnp.where(i == 0, 2, jnp.where(i == 1, 1, jnp.where(i == 2, 3, 0)))
         attend_pair(
             lax.rem(z + o, 4), slab, rope_even, rope_odd, bias, q_ref, wuk_ref, wuv_ref,
-            keys, values, parts,
+            keys, values, parts1, parts2,
         )
         for a, b in ((1, 0), (1, 1), (0, 1)):
-            spread(o, a, b).start()
+            spread(0, o, a, b).start()
 
         @pl.when(o != 0)
         def _():
-            spread(o, 0, 0).start()
+            spread(0, o, 0, 0).start()
 
         return carry
 
-    lax.fori_loop(0, PAIRS, attend_step, 0)
-    own_part.start()
     ways = [(o, a, b) for o in (2, 1, 3, 0) for a in (1, 0) for b in (1, 0)]
     others = [way for way in ways if way != (0, 0, 0)]
-    for way in others:
-        spread(*way).wait_recv()
-    own_part.wait()
+
+    def spread_second(a):
+        for way in others:
+            if way[1] == a:
+                spread(1, *way).start()
+
+    def spread_done(g):
+        for way in others:
+            spread(g, *way).wait_recv()
+        own_part(g).wait()
+
+    lax.fori_loop(0, PAIRS, attend_step, 0)
+    own_part(0).start()
+    own_part(1).start()
+    spread_second(1)
+    spread_done(0)
 
     part = 2 * core + hi
     staged_near, staged_far = (staged_near1, staged_near2), (staged_far1, staged_far2)
@@ -274,7 +319,7 @@
 
     def taken(rank, e, u):
         source = lax.rem(rank + DP - off_ref[block_of(part, e, u)], DP)
-        return gathered[source, e, u]
+        return gathered2[source, e, u - 1] if u else gathered1[source, e, 0]
 
     def deliver(g, o, a, b):
         at = g * DP + o * 4 + a * 2 + b
@@ -282,7 +327,9 @@
         dst = (far if a else near)[g].at[2 * z + core]
         return remote(src, dst, p2_s.at[at], p2_r.at[at], rank_at(o, a, b), tp)
 
-    for g, units in enumerate(((0,), (1, 2))):
+    def deliver_all(g):
+        units = ((0,), (1, 2))[g]
+        count = len(units)
         for o, a, b in ways:
             rank = rank_at(o, a, b)
             own = (o, a, b) == (0, 0, 0)
@@ -292,7 +339,6 @@
                 target, index = near[g], 2 * z + core
             else:
                 target, index = staged_near[g], 2 * o + b
-            count = len(units)
             for n, u in enumerate(units):
                 target[index, n] = taken(rank, lo, u)
             if not a:
@@ -307,6 +353,8 @@
     def arrived(g):
         for way in others:
             deliver(g, *way).wait_recv()
+        if g == 0:
+            spread_second(0)
         count = g + 1
         for pair in range(PAIRS):
             columns = pl.ds(pair * PART, PART)
@@ -368,8 +416,25 @@
     def y2_copies(t, c):
         return y_copies(t, c, t.y2_out, t.y2_in, y2s_sem, y2r_sem)
 
-    def sums(t, slot, at):
-        return t.acc[slot, pl.ds(t.count * at, t.count)].reshape(t.rows, CHUNK)
+    def sums(t, c, at, over_x):
+        own = t.acc[lax.rem(c, t.lags[2] + 1), pl.ds(t.count * at, t.count)].astype(F32)
+        if over_x:
+            units = []
+            for n in range(t.count):
+                places = HOLDS[t.g]
+                side = choose(at, [places[i][n][0] for i in range(4)])
+                place = choose(at, [places[i][n][1] for i in range(4)])
+                units.append(t.x_in[c, side, place].astype(F32))
+            own = own + jnp.stack(units)
+        return own.reshape(t.rows, CHUNK)
+
+    def either_way(t, c, body):
+        if t.g == 0:
+            body(True)
+        else:
+            over_x = goes_over_x(t, c, hi)
+            pl.when(over_x)(lambda: body(True))
+            pl.when(jnp.logical_not(over_x))(lambda: body(False))
 
     def multiply(t, i):
         c = i - t.g * CHUNKS
@@ -389,7 +454,7 @@
             t.x_out[c] = both[: 4 * UNIT].astype(BF16).reshape(2, 2, UNIT, CHUNK)
             for copy in x_copies(t, c):
                 copy.start()
-            t.acc[at] = both[4 * UNIT :].reshape(4, UNIT, CHUNK)
+            t.acc[at] = both[4 * UNIT :].astype(BF16).reshape(4, UNIT, CHUNK)
         else:
             t.x_out[c] = (
                 jnp.dot(away2[...].reshape(8 * UNIT, TP * VH), w, preferred_element_type=F32)
@@ -398,12 +463,20 @@
             )
             start_x(t, c)
             start_y_first(t, c)
-            t.acc[at] = jnp.dot(
-                keep2[...].reshape(8 * UNIT, TP * VH), w, preferred_element_type=F32
-            ).reshape(8, UNIT, CHUNK)
+            t.acc[at] = (
+                jnp.dot(keep2[...].reshape(8 * UNIT, TP * VH), w, preferred_element_type=F32)
+                .astype(BF16)
+                .reshape(8, UNIT, CHUNK)
+            )
+
+    def y_first(c):
+        return (lax.rem(c, 2) == 0) & (c < 2 * Y_FIRST)
+
+    def y_side(c):
+        return lax.rem(c // 2, 2)
 
     def goes_over_x(t, c, to):
-        return (c >= Y_FIRST) | (lax.rem(c, 2) != to)
+        return jnp.logical_not(y_first(c)) | (y_side(c) != to)
 
     def start_x(t, c):
         for a, copy in enumerate(x_copies(t, c)):
@@ -411,30 +484,33 @@
 
     def away_unit(c, to):
         at = choose(3 - to, [jnp.where(hi == 0, AWAY[0][i], AWAY[1][i]) for i in range(4)])
-        return x_out2[c, lax.rem(c, 2), at]
+        return x_out2[c, y_side(c), at]
 
     def a1_copies(c):
+        c = c // 2
         return [
             remote(a1_out.at[c, a], a1_in.at[c, a], a1s_sem.at[c, a], a1r_sem.at[c, a], dp, to)
             for a, to in enumerate((up, down))
         ]
 
     def a2_copies(c):
+        c = c // 2
         return [
             remote(a2_out.at[c, a], a2_in.at[c, a], a2s_sem.at[c, a], a2r_sem.at[c, a], dp, to)
             for a, to in enumerate((up, down))
         ]
 
     def x2_copy(c):
-        rank = lax.rem(c, 2) * 8 + 2 * z + core
+        rank = y_side(c) * 8 + 2 * z + core
+        c = c // 2
         return remote(x2_out.at[c], x2_in.at[c, hi], x2s_sem.at[c], x2r_sem.at[c, hi], rank, across)
 
     def start_y_first(t, c):
-        @pl.when(c < Y_FIRST)
+        @pl.when(y_first(c))
         def _():
             other = away_unit(c, far_y)
-            a1_out[c, 0] = other[:, :HALF]
-            a1_out[c, 1] = other[:, HALF:]
+            a1_out[c // 2, 0] = other[:, :HALF]
+            a1_out[c // 2, 1] = other[:, HALF:]
             for copy in a1_copies(c):
                 copy.start()
 
@@ -442,14 +518,14 @@
         for copy in a1_copies(c):
             copy.wait_recv()
         to_up = away_unit(c, up_y)
-        a2_out[c, 0, :, :HALF] = (
-            to_up[:, :HALF].astype(F32) + a1_in[c, 0].astype(F32)
+        a2_out[c // 2, 0, :, :HALF] = (
+            to_up[:, :HALF].astype(F32) + a1_in[c // 2, 0].astype(F32)
         ).astype(BF16)
-        a2_out[c, 0, :, HALF:] = to_up[:, HALF:]
+        a2_out[c // 2, 0, :, HALF:] = to_up[:, HALF:]
         to_down = away_unit(c, down_y)
-        a2_out[c, 1, :, :HALF] = to_down[:, :HALF]
-        a2_out[c, 1, :, HALF:] = (
-            to_down[:, HALF:].astype(F32) + a1_in[c, 1].astype(F32)
+        a2_out[c // 2, 1, :, :HALF] = to_down[:, :HALF]
+        a2_out[c // 2, 1, :, HALF:] = (
+            to_down[:, HALF:].astype(F32) + a1_in[c // 2, 1].astype(F32)
         ).astype(BF16)
         for copy in a2_copies(c):
             copy.start()
@@ -457,53 +533,45 @@
     def after_a2(t, c):
         for copy in a2_copies(c):
             copy.wait_recv()
-        x2_out[c] = (
-            away_unit(c, own_y).astype(F32) + a2_in[c, 0].astype(F32) + a2_in[c, 1].astype(F32)
+        x2_out[c // 2] = (
+            away_unit(c, own_y).astype(F32) + a2_in[c // 2, 0].astype(F32) + a2_in[c // 2, 1].astype(F32)
         ).astype(BF16)
         x2_copy(c).start()
 
-    def add_x(t, c):
-        slot = lax.rem(c, t.lags[2] + 1)
-        for copy in x_copies(t, c):
-            copy.wait_recv()
-        for side in range(2):
-            for half in range(2):
-                for n in range(t.count):
-                    p = 2 * half + side
-                    home = SECOND[p][n] if t.g else FIRST[p]
-                    t.acc[slot, home] = t.acc[slot, home] + t.x_in[
-                        c, side, t.count * half + n
-                    ].astype(F32)
-
     def after_x(t, c):
-        if t.g == 0:
-            add_x(t, c)
-        else:
-            pl.when(goes_over_x(t, c, hi))(lambda: add_x(t, c))
-        slot = lax.rem(c, t.lags[2] + 1)
-        other = sums(t, slot, far_y).astype(BF16)
-        t.y1_out[c, 0] = other[:, :HALF]
-        t.y1_out[c, 1] = other[:, HALF:]
+        def body(over_x):
+            if over_x:
+                for copy in x_copies(t, c):
+                    copy.wait_recv()
+            other = sums(t, c, far_y, over_x).astype(BF16)
+            t.y1_out[c, 0] = other[:, :HALF]
+            t.y1_out[c, 1] = other[:, HALF:]
+
+        either_way(t, c, body)
         for copy in y1_copies(t, c):
             copy.start()
 
     def after_y1(t, c):
-        slot = lax.rem(c, t.lags[2] + 1)
         for copy in y1_copies(t, c):
             copy.wait_recv()
-        to_up = sums(t, slot, up_y)
-        t.y2_out[c, 0, :, :HALF] = (to_up[:, :HALF] + t.y1_in[c, 0].astype(F32)).astype(BF16)
-        t.y2_out[c, 0, :, HALF:] = to_up[:, HALF:].astype(BF16)
-        to_down = sums(t, slot, down_y)
-        t.y2_out[c, 1, :, :HALF] = to_down[:, :HALF].astype(BF16)
-        t.y2_out[c, 1, :, HALF:] = (to_down[:, HALF:] + t.y1_in[c, 1].astype(F32)).astype(BF16)
+
+        def body(over_x):
+            to_up = sums(t, c, up_y, over_x)
+            t.y2_out[c, 0, :, :HALF] = (to_up[:, :HALF] + t.y1_in[c, 0].astype(F32)).astype(BF16)
+            t.y2_out[c, 0, :, HALF:] = to_up[:, HALF:].astype(BF16)
+            to_down = sums(t, c, down_y, over_x)
+            t.y2_out[c, 1, :, :HALF] = to_down[:, :HALF].astype(BF16)
+            t.y2_out[c, 1, :, HALF:] = (
+                to_down[:, HALF:] + t.y1_in[c, 1].astype(F32)
+            ).astype(BF16)
+
+        either_way(t, c, body)
         for copy in y2_copies(t, c):
             copy.start()
 
     edge = (own_y == 0) | (own_y == 3)
 
     def after_y2(t, c):
-        slot = lax.rem(c, t.lags[2] + 1)
         for copy in y2_copies(t, c):
             copy.wait_recv()
         start = pl.multiple_of(c * CHUNK, CHUNK)
@@ -512,31 +580,25 @@
         else:
             thirds = [0, jnp.where(edge, 1, 2)]
 
-        def finish(more):
-            total = sums(t, slot, own_y) + t.y2_in[c, 0].astype(F32) + t.y2_in[c, 1].astype(F32)
+        def body(over_x):
+            if not over_x:
+                for side in range(2):
+                    remote(
+                        x2_out.at[c // 2], x2_in.at[c // 2, side], x2s_sem.at[c // 2],
+                        x2r_sem.at[c // 2, side], dp, across,
+                    ).wait_recv()
+            total = sums(t, c, own_y, over_x)
+            total = total + t.y2_in[c, 0].astype(F32) + t.y2_in[c, 1].astype(F32)
             for n, third in enumerate(thirds):
                 unit = total[n * UNIT : (n + 1) * UNIT]
-                if more:
+                if not over_x:
                     side = jnp.where(own_y == 0, 1 - n, n)
-                    unit = unit + x2_in[c, side].astype(F32)
+                    unit = unit + x2_in[c // 2, side].astype(F32)
                 out_ref[jnp.where(lo == 1, 2 - third, third), :, pl.ds(start, CHUNK)] = (
                     unit.astype(BF16)
                 )
 
-        if t.g == 0:
-            finish(False)
-        else:
-            over_x = goes_over_x(t, c, hi)
-            pl.when(over_x)(lambda: finish(False))
-
-            @pl.when(jnp.logical_not(over_x))
-            def _():
-                for side in range(2):
-                    remote(
-                        x2_out.at[c], x2_in.at[c, side], x2s_sem.at[c], x2r_sem.at[c, side],
-                        dp, across,
-                    ).wait_recv()
-                finish(True)
+        either_way(t, c, body)
 
     def later(t, i, least, most):
         for lag, stage in zip(t.lags, (after_x, after_y1, after_y2)):
@@ -551,7 +613,7 @@
             for lag, stage in zip(t.lags[:2], (after_a1, after_a2)):
                 low = CHUNKS + lag
 
-                @pl.when((i >= low) & (i < low + Y_FIRST))
+                @pl.when((i >= low) & y_first(i - low))
                 def _(stage=stage, low=low):
                     stage(t, i - low)
 
@@ -570,8 +632,12 @@
         later(groups[1], i, STEPS, STEPS + LAGS[1][2])
         return carry
 
+    deliver_all(0)
     arrived(0)
-    lax.fori_loop(0, CHUNKS, first_step, 0)
+    lax.fori_loop(0, DELIVER_AT, first_step, 0)
+    spread_done(1)
+    deliver_all(1)
+    lax.fori_loop(DELIVER_AT, CHUNKS, first_step, 0)
     arrived(1)
     lax.fori_loop(CHUNKS, STEPS, second_step, 0)
     lax.fori_loop(STEPS, STEPS + LAGS[1][2], last_step, 0)
@@ -579,7 +645,8 @@
     for copy in gathers:
         copy.wait_send()
     for way in others:
-        spread(*way).wait_send()
+        spread(0, *way).wait_send()
+        spread(1, *way).wait_send()
         deliver(0, *way).wait_send()
         deliver(1, *way).wait_send()
 
@@ -592,7 +659,7 @@
         for a, copy in enumerate(x_copies(groups[1], c)):
             pl.when(goes_over_x(groups[1], c, flip(hi, a)))(copy.wait_send)
 
-        @pl.when(c < Y_FIRST)
+        @pl.when(y_first(c))
         def _():
             for copy in a1_copies(c) + a2_copies(c) + [x2_copy(c)]:
                 copy.wait_send()
@@ -605,7 +672,7 @@
 def sum_scratch(g):
     rows = GROUPS[g] * UNIT
     return [
-        pltpu.VMEM((LAGS[g][2] + 1, 4 * GROUPS[g], UNIT, CHUNK), F32),
+        pltpu.VMEM((LAGS[g][2] + 1, 4 * GROUPS[g], UNIT, CHUNK), BF16),
         pltpu.VMEM((CHUNKS, 2, 2 * GROUPS[g], UNIT, CHUNK), BF16),
         pltpu.VMEM((CHUNKS, 2, 2 * GROUPS[g], UNIT, CHUNK), BF16),
         pltpu.VMEM((CHUNKS, 2, rows, HALF), BF16),
@@ -633,9 +700,11 @@
             pltpu.VMEM((ROWS, 2 * ROPE), BF16),
             pltpu.VMEM((NB, BLK, WINDOW * BLK), F32),
             pltpu.VMEM((2, ROWS, 2 * NOPE), BF16),
-            pltpu.VMEM((ROWS, 2 * VH), BF16),
-            pltpu.VMEM((PAIRS, PARTS, 2, 3, UNIT, PART), BF16),
-            pltpu.VMEM((DP, 2, 3, UNIT, PART), BF16),
+            pltpu.VMEM((2, ROWS, 2 * VH), BF16),
+            pltpu.VMEM((PAIRS, PARTS, 2, 1, UNIT, PART), BF16),
+            pltpu.VMEM((PAIRS, PARTS, 2, 2, UNIT, PART), BF16),
+            pltpu.VMEM((DP, 2, 1, UNIT, PART), BF16),
+            pltpu.VMEM((DP, 2, 2, UNIT, PART), BF16),
             pltpu.VMEM((8, 3, UNIT, PART), BF16),
             pltpu.VMEM((8, 6, UNIT, PART), BF16),
             pltpu.VMEM((8, 1, UNIT, PART), BF16),
@@ -661,8 +730,8 @@
             dma((4,)),
             dma((TP - 1,)),
             dma((TP - 1,)),
-            dma((DP,)),
-            dma((DP,)),
+            dma((2 * DP,)),
+            dma((2 * DP,)),
             dma((2 * DP,)),
             dma((2 * DP,)),
             dma((W_SLOTS,)),
@@ -674,7 +743,7 @@
             collective_id=0, has_side_effects=True, vmem_limit_bytes=58 * 2**20
         ),
         name="whole",
-    )(segments, offsets, latent, queries, w_uk, w_uv, w_out)
+    )(segments.T, offsets, latent, queries, w_uk, w_uv, w_out)
     return out.reshape(OWN, D)
 
 

time: 130 us -> 126 us (0.969)
  Pallas kernels: 126 us -> 123 us
  local copies, waits for them, and re-layouts: 3.87 us -> 2.51 us
    pallas_call x1, Pallas kernels: 126 us -> 123 us  [on_device(): pl.pallas_call(whole_kernel, out_shape=jax.ShapeDtypeStruct((3, UNIT, D),...]
    unnamed x2 -> x1, local copies, waits for them, and re-layouts: 3.87 us -> 2.51 us
where the time goes in v5:
time: 126 us; the launch traced here: 125 us
  Pallas kernels  123 us (98%)
  local copies, waits for them, and re-layouts  2.51 us (2%)
    pallas_call x1, Pallas kernels, on_device(): pl.pallas_call(whole_kernel, out_shape=jax.ShapeDtypeStruct((3, UNIT, D),...  123 us

profile of v5, /device:TPU:0, one launch (start us, length us, event | category | flops | bytes accessed | tf_op | source)
XLA Modules:
  0.0 125.5 jit_solution(1601689375938418154)
XLA Ops:
  0.0 123.0 %whole.1 = bf16[3,32,7168]{2,1,0:T(8,128)(2,1)} custom-call(s32[6,16]{1,0:T(8,128)} %bitcast.3, s32[6]{0:T(128)} %off_ref.1, bf16[96,576]{1,0:T(8,128)(2,1)} %lat_hbm.1, bf16[768,1536]{1,0:T(8,128)(2,1)} %q_hbm.1, bf16[8,128,512]{2,1,0:T(8,128)(2,1)} %wuk_hbm.1, bf16[8,512,128]{2,1,0:T(8,128)(2,1)} %wuv_hbm.1, bf16[1024,7168]{1,0:T(8,128)(2,1)} %w_hbm.1), custom_call_target="tpu_custom_call" | custom-call | tf_op jit(solution)/shard_map/whole/pallas_call | solution.py:689
  123.0 2.5 %copy.9 = bf16[96,7168]{1,0:T(8,128)(2,1)} copy(bf16[96,7168]{1,0:T(8,128)(2,1)} %bitcast.2) | data formatting | bytes 2752512

commit v6 on v5

--- a/solution.py
+++ b/solution.py
@@ -36,7 +36,7 @@
 GROUPS = (1, 2)
 LAGS = ((4, 7, 10), (3, 5, 8))
 Y_FIRST = 5
-AHEAD = 3
+AHEAD = 5
 DELIVER_AT = 5
 
 MESH = pl.DeviceIdType.MESH
@@ -310,7 +310,6 @@
     lax.fori_loop(0, PAIRS, attend_step, 0)
     own_part(0).start()
     own_part(1).start()
-    spread_second(1)
     spread_done(0)
 
     part = 2 * core + hi
@@ -633,6 +632,7 @@
         return carry
 
     deliver_all(0)
+    spread_second(1)
     arrived(0)
     lax.fori_loop(0, DELIVER_AT, first_step, 0)
     spread_done(1)

time: 126 us -> 124 us (0.984)
  Pallas kernels: 123 us -> 121 us
    pallas_call x1, Pallas kernels: 123 us -> 121 us  [on_device(): pl.pallas_call(whole_kernel, out_shape=jax.ShapeDtypeStruct((3, UNIT, D),...]
where the time goes in v6:
time: 124 us
  Pallas kernels  121 us (98%)
  local copies, waits for them, and re-layouts  2.51 us (2%)
    pallas_call x1, Pallas kernels, on_device(): pl.pallas_call(whole_kernel, out_shape=jax.ShapeDtypeStruct((3, UNIT, D),...  121 us
    unnamed x1, local copies, waits for them, and re-layouts  2.51 us

profile of v6, /device:TPU:0, one launch (start us, length us, event | category | flops | bytes accessed | tf_op | source)
XLA Modules:
  0.0 123.8 jit_solution(15989473170285849345)
XLA Ops:
  0.0 121.3 %whole.1 = bf16[3,32,7168]{2,1,0:T(8,128)(2,1)} custom-call(s32[6,16]{1,0:T(8,128)} %bitcast.3, s32[6]{0:T(128)} %off_ref.1, bf16[96,576]{1,0:T(8,128)(2,1)} %lat_hbm.1, bf16[768,1536]{1,0:T(8,128)(2,1)} %q_hbm.1, bf16[8,128,512]{2,1,0:T(8,128)(2,1)} %wuk_hbm.1, bf16[8,512,128]{2,1,0:T(8,128)(2,1)} %wuv_hbm.1, bf16[1024,7168]{1,0:T(8,128)(2,1)} %w_hbm.1), custom_call_target="tpu_custom_call" | custom-call | tf_op jit(solution)/shard_map/whole/pallas_call | solution.py:689
  121.3 2.5 %copy.9 = bf16[96,7168]{1,0:T(8,128)(2,1)} copy(bf16[96,7168]{1,0:T(8,128)(2,1)} %bitcast.2) | data formatting | bytes 2752512

commit v7 on v6

--- a/solution.py
+++ b/solution.py
@@ -179,16 +179,16 @@
 
 
 def whole_kernel(
-    seg_ref, off_ref, lat_hbm, q_hbm, wuk_hbm, wuv_hbm, w_hbm, out_ref,
+    seg_ref, off_ref, lat_hbm, q_hbm, wuk_hbm, wuv_hbm, w_hbm, out_hbm,
     slab, q_ref, wuk_ref, wuv_ref, rope_even, rope_odd, bias, keys, values,
     parts1, parts2, gathered1, gathered2, staged_near1, staged_near2, staged_far1, staged_far2, near1, near2, far1, far2,
     rows1, keep2, away2, w_buf,
     acc1, x_out1, x_in1, y1_out1, y1_in1, y2_out1, y2_in1,
     acc2, x_out2, x_in2, y1_out2, y1_in2, y2_out2, y2_in2,
-    a1_out, a1_in, a2_out, a2_in, x2_out, x2_in,
+    a1_out, a1_in, a2_out, a2_in, x2_out, x2_in, out_ref,
     own_sem, ag_s, ag_r, p1_s, p1_r, p2_s, p2_r,
     w_sem, xs_sem, xr_sem, y1s_sem, y1r_sem, y2s_sem, y2r_sem,
-    a1s_sem, a1r_sem, a2s_sem, a2r_sem, x2s_sem, x2r_sem,
+    a1s_sem, a1r_sem, a2s_sem, a2r_sem, x2s_sem, x2r_sem, out_sem,
 ):
     dp, tp = ranks()
     y, lo = tp // 2, lax.rem(tp, 2)
@@ -570,14 +570,25 @@
 
     edge = (own_y == 0) | (own_y == 3)
 
+    def thirds_of(t):
+        thirds = [0, jnp.where(edge, 1, 2)] if t.g else [jnp.where(edge, 2, 1)]
+        return [jnp.where(lo == 1, 2 - third, third) for third in thirds]
+
+    def out_copies(t, c):
+        columns = pl.ds(pl.multiple_of(c * CHUNK, CHUNK), CHUNK)
+        return [
+            pltpu.make_async_copy(
+                out_ref.at[third, :, columns], out_hbm.at[third, :, columns],
+                out_sem.at[c, t.g + n],
+            )
+            for n, third in enumerate(thirds_of(t))
+        ]
+
     def after_y2(t, c):
         for copy in y2_copies(t, c):
             copy.wait_recv()
         start = pl.multiple_of(c * CHUNK, CHUNK)
-        if t.g == 0:
-            thirds = [jnp.where(edge, 2, 1)]
-        else:
-            thirds = [0, jnp.where(edge, 1, 2)]
+        thirds = thirds_of(t)
 
         def body(over_x):
             if not over_x:
@@ -593,11 +604,13 @@
                 if not over_x:
                     side = jnp.where(own_y == 0, 1 - n, n)
                     unit = unit + x2_in[c // 2, side].astype(F32)
-                out_ref[jnp.where(lo == 1, 2 - third, third), :, pl.ds(start, CHUNK)] = (
+                out_ref[third, :, pl.ds(start, CHUNK)] = (
                     unit.astype(BF16)
                 )
 
         either_way(t, c, body)
+        for copy in out_copies(t, c):
+            copy.start()
 
     def later(t, i, least, most):
         for lag, stage in zip(t.lags, (after_x, after_y1, after_y2)):
@@ -654,6 +667,8 @@
         for t in groups:
             for copy in y1_copies(t, c) + y2_copies(t, c):
                 copy.wait_send()
+            for copy in out_copies(t, c):
+                copy.wait()
         for copy in x_copies(groups[0], c):
             copy.wait_send()
         for a, copy in enumerate(x_copies(groups[1], c)):
@@ -690,7 +705,7 @@
         whole_kernel,
         out_shape=jax.ShapeDtypeStruct((3, UNIT, D), BF16),
         in_specs=[smem_spec] * 2 + [any_spec] * 5,
-        out_specs=pl.BlockSpec(memory_space=pltpu.VMEM),
+        out_specs=any_spec,
         scratch_shapes=[
             pltpu.VMEM((TP, OWN, KV), BF16),
             pltpu.VMEM((ROWS, HEADS * (NOPE + ROPE)), BF16),
@@ -727,6 +742,7 @@
             pltpu.VMEM((Y_FIRST, 2, UNIT, CHUNK), BF16),
             pltpu.VMEM((Y_FIRST, UNIT, CHUNK), BF16),
             pltpu.VMEM((Y_FIRST, 2, UNIT, CHUNK), BF16),
+            pltpu.VMEM((3, UNIT, D), BF16),
             dma((4,)),
             dma((TP - 1,)),
             dma((TP - 1,)),
@@ -738,7 +754,7 @@
         ]
         + [dma((STEPS, 2))] * 6
         + [dma((Y_FIRST, 2))] * 4
-        + [dma((Y_FIRST,)), dma((Y_FIRST, 2))],
+        + [dma((Y_FIRST,)), dma((Y_FIRST, 2)), dma((CHUNKS, 3))],
         compiler_params=pltpu.CompilerParams(
             collective_id=0, has_side_effects=True, vmem_limit_bytes=58 * 2**20
         ),

time: 124 us -> 123 us (level)
  no operation moved by 1% of the time
where the time goes in v7:
time: 123 us
  Pallas kernels  121 us (98%)
  local copies, waits for them, and re-layouts  2.51 us (2%)
    pallas_call x1, Pallas kernels, on_device(): pl.pallas_call(whole_kernel, out_shape=jax.ShapeDtypeStruct((3, UNIT, D),...  121 us
    unnamed x1, local copies, waits for them, and re-layouts  2.51 us

profile of v7, /device:TPU:0, one launch (start us, length us, event | category | flops | bytes accessed | tf_op | source)
XLA Modules:
  0.0 123.2 jit_solution(3534382930172013814)
XLA Ops:
  0.0 120.7 %whole.1 = bf16[3,32,7168]{2,1,0:T(8,128)(2,1)} custom-call(s32[6,16]{1,0:T(8,128)} %bitcast.3, s32[6]{0:T(128)} %off_ref.1, bf16[96,576]{1,0:T(8,128)(2,1)} %lat_hbm.1, bf16[768,1536]{1,0:T(8,128)(2,1)} %q_hbm.1, bf16[8,128,512]{2,1,0:T(8,128)(2,1)} %wuk_hbm.1, bf16[8,512,128]{2,1,0:T(8,128)(2,1)} %wuv_hbm.1, bf16[1024,7168]{1,0:T(8,128)(2,1)} %w_hbm.1), custom_call_target="tpu_custom_call" | custom-call | tf_op jit(solution)/shard_map/whole/pallas_call | solution.py:704
  120.7 2.5 %copy.9 = bf16[96,7168]{1,0:T(8,128)(2,1)} copy(bf16[96,7168]{1,0:T(8,128)(2,1)} %bitcast.2) | data formatting | bytes 2752512

commit v8 on v7

--- a/solution.py
+++ b/solution.py
@@ -225,9 +225,9 @@
         load(c).start()
 
     greet(
-        [(dp, lax.rem(tp + o, TP)) for o in range(1, TP)]
-        + [(lax.rem(dp + o, DP), tp) for o in range(1, DP)]
-        + [(lax.rem(dp + DP // 2, DP), across)]
+        [(lax.rem(dp + DP // 2, DP), across)]
+        + [(lax.rem(dp + o, DP), tp) for o in range(DP - 1, 0, -1)]
+        + [(dp, lax.rem(tp + o, TP)) for o in (4, 5, 3, 6, 2, 7, 1)]
     )
 
     opposite = 2 * lax.rem(y + 2, 4) + lo
@@ -635,8 +635,8 @@
         return carry
 
     def second_step(i, carry):
+        later(groups[0], i, CHUNKS, STEPS)
         multiply(groups[1], i)
-        later(groups[0], i, CHUNKS, STEPS)
         later(groups[1], i, CHUNKS, STEPS)
         return carry
 

time: 123 us -> 124 us (level)
  no operation moved by 1% of the time
where the time goes in v8:
time: 124 us; the launch traced here: 123 us
  Pallas kernels  121 us (98%)
  local copies, waits for them, and re-layouts  2.51 us (2%)
    pallas_call x1, Pallas kernels, on_device(): pl.pallas_call(whole_kernel, out_shape=jax.ShapeDtypeStruct((3, UNIT, D),...  121 us
    unnamed x1, local copies, waits for them, and re-layouts  2.51 us

profile of v8, /device:TPU:0, one launch (start us, length us, event | category | flops | bytes accessed | tf_op | source)
XLA Modules:
  0.0 123.4 jit_solution(15745665185297263911)
XLA Ops:
  0.0 120.9 %whole.1 = bf16[3,32,7168]{2,1,0:T(8,128)(2,1)} custom-call(s32[6,16]{1,0:T(8,128)} %bitcast.3, s32[6]{0:T(128)} %off_ref.1, bf16[96,576]{1,0:T(8,128)(2,1)} %lat_hbm.1, bf16[768,1536]{1,0:T(8,128)(2,1)} %q_hbm.1, bf16[8,128,512]{2,1,0:T(8,128)(2,1)} %wuk_hbm.1, bf16[8,512,128]{2,1,0:T(8,128)(2,1)} %wuv_hbm.1, bf16[1024,7168]{1,0:T(8,128)(2,1)} %w_hbm.1), custom_call_target="tpu_custom_call" | custom-call | tf_op jit(solution)/shard_map/whole/pallas_call | solution.py:704
  120.9 2.5 %copy.9 = bf16[96,7168]{1,0:T(8,128)(2,1)} copy(bf16[96,7168]{1,0:T(8,128)(2,1)} %bitcast.2) | data formatting | bytes 2752512
